TPU v7x, 32 devices: a whole 2x2x4 slice. The times are simulated.
32 devices in a mesh: grp: 4 (over x, core), tile: 8 (over z, y).
Axes of the slice: x: 2, y: 2, z: 4, core: 2. Of those that a mesh axis runs over, the one named last changes fastest.
Arguments:
- tx_fields: bfloat16 [64, 8192], P(None, 'tile'), may hold values from -6 to 6
- rx_fields: bfloat16 [128, 8192], P(None, 'tile'), may hold values from -6 to 6
- layer_of_cell: int32 [8192], P('tile'), may hold values from 0 to 31
- layer_cond: float32 [32], replicated, may hold values from 0.05 to 5
- tx_of_row: int32 [1408], replicated, may hold values from 0 to 63
- rx_of_row: int32 [1408], replicated, may hold values from 0 to 127
- damping: float32 [1408], replicated, may hold values from 0.5 to 5
- panel_order: int32 [1408], replicated, may hold values from 0 to 1407, each once
Outputs:
- trailing: float32 [1408, 1408], P('grp', 'tile')
- factor: float32 [1408, 1024], P('grp')
Inputs may be any that keep to these rules, and one draw needn't show every extreme that they name: `panel_order`: each data row appears exactly once; panel k is entries k * 512 to (k + 1) * 512 - 1.
All inputs are finite; a program needn't handle non-finite values.
Results may differ from a plain program's by a relative error of at most 0.0014.
Values may be sent and summed in bfloat16 or wider, within the bound.
No kernel may reach another device: no remote copies, remote signals or barrier semaphores. Data moves between devices by JAX's collectives and lax.ppermute only.
A program may use at most 64 MiB of HBM per device.

v0:
```python
import functools

import jax
import jax.numpy as jnp
from jax import lax
from jax.experimental import pallas as pl
from jax.experimental.pallas import tpu as pltpu
from jax.sharding import PartitionSpec as P

PANEL = 512
NPAN = 2
BLOCK = 128
STEP = 16
STRIP = 256
PARTS = 4
GROUP = 3
PAD = 16
VMEM = pl.BlockSpec(memory_space=pltpu.VMEM)
SMEM = pl.BlockSpec(memory_space=pltpu.SMEM)
ROWS_ROWS = ((1,), (1,))
PLAIN = ((1,), (0,))


def grant(*shapes):
    total = 0
    for shape, width in shapes:
        size = width
        for axis in shape:
            size *= axis
        total += size
    return min(60 * 2**20, total + total // 8 + 6 * 2**20)


def halves(value):
    high = value.astype(jnp.bfloat16)
    low = (value - high.astype(jnp.float32)).astype(jnp.bfloat16)
    return high, low


def dot(a, b, dims):
    return lax.dot_general(a, b, (dims, ((), ())), preferred_element_type=jnp.float32)


def product(left, right, dims):
    return dot(left[0], right[0], dims) + (dot(left[0], right[1], dims) + dot(left[1], right[0], dims))


def factor_block(block, work, upper, beside=()):
    size = block.shape[0]
    row = lax.broadcasted_iota(jnp.int32, (size, size), 0)
    col = lax.broadcasted_iota(jnp.int32, (size, size), 1)
    eye = (row == col).astype(jnp.float32)
    work[:, :size] = block
    work[:, size:] = eye
    sub = lax.broadcasted_iota(jnp.int32, (STEP, size), 0)
    wide = (STEP, size)
    rows0, rows1 = block[:STEP, :], eye[:STEP, :]
    for at in range(0, size, STEP):
        cols = [jnp.broadcast_to(rows0[:, at + k : at + k + 1], wide) for k in range(STEP)]
        for call in beside[at * len(beside) // size : (at + STEP) * len(beside) // size]:
            call()
        more = at + STEP < size
        if more:
            after = work[at + STEP : at + 2 * STEP, :]
            after_cols = [jnp.broadcast_to(after[:, at + k : at + k + 1], wide) for k in range(STEP)]
        done0 = done1 = jnp.zeros(wide, jnp.float32)
        for j in range(STEP):
            pivot = jnp.broadcast_to(cols[j][j : j + 1, :], wide)
            ratio = (cols[j] - jnp.where(sub == j, 1.0, 0.0)) * (1.0 / pivot)
            root = lax.rsqrt(pivot)
            row0 = jnp.broadcast_to(rows0[j : j + 1, :], wide)
            row1 = jnp.broadcast_to(rows1[j : j + 1, :], wide)
            done0 = jnp.where(sub == j, row0 * root, done0)
            done1 = jnp.where(sub == j, row1 * root, done1)
            rows0 = rows0 - ratio * row0
            rows1 = rows1 - ratio * row1
            for k in range(j + 1, STEP):
                cols[k] = cols[k] - ratio * jnp.broadcast_to(cols[k][j : j + 1, :], wide)
        upper[at : at + STEP, :size] = done0
        upper[at : at + STEP, size:] = done1
        if not more:
            break
        terms0 = [after_cols[k] * jnp.broadcast_to(rows0[k : k + 1, :], wide) for k in range(STEP)]
        terms1 = [after_cols[k] * jnp.broadcast_to(rows1[k : k + 1, :], wide) for k in range(STEP)]
        while len(terms0) > 1:
            terms0 = [a + b for a, b in zip(terms0[::2], terms0[1::2])]
            terms1 = [a + b for a, b in zip(terms1[::2], terms1[1::2])]
        if at + 2 * STEP < size:
            solved = jnp.concatenate([rows0, rows1], axis=1)
            parts = [solved, jnp.zeros((size - at - STEP, 2 * size), jnp.float32)]
            if at > 0:
                parts.insert(0, jnp.zeros((at, 2 * size), jnp.float32))
            rest = work[at + 2 * STEP :, :]
            work[at + 2 * STEP :, :] = rest - product(
                halves(rest[:, :size]), halves(jnp.concatenate(parts, axis=0)), PLAIN
            )
        rows0 = after[:, :size] - terms0[0]
        rows1 = after[:, size:] - terms1[0]


def strips_of(rows):
    return [(a, min(a + STRIP, rows)) for a in range(0, rows, STRIP)]


def select_body(ntx, nrx, order, tx_of_row, rx_of_row, damping, hot, damp, line, table):
    rows = order.shape[0]
    table[:ntx, :] = (
        lax.broadcasted_iota(jnp.int32, (ntx, rows), 0) == tx_of_row[...].reshape(1, rows)
    ).astype(jnp.bfloat16)
    table[ntx : ntx + nrx, :] = (
        lax.broadcasted_iota(jnp.int32, (nrx, rows), 0) == rx_of_row[...].reshape(1, rows)
    ).astype(jnp.bfloat16)
    line[...] = order[...].reshape(1, rows)
    spare = table.shape[0] - ntx - nrx
    damping = damping[...].reshape(1, rows)
    high = damping.astype(jnp.bfloat16).astype(jnp.float32)
    middle, low = halves(damping - high)
    which = lax.broadcasted_iota(jnp.int32, (spare, rows), 0)
    table[ntx + nrx :, :] = (
        jnp.where(which == 0, high, 0.0)
        + jnp.where(which == 1, middle.astype(jnp.float32), 0.0)
        + jnp.where(which == 2, low.astype(jnp.float32), 0.0)
    ).astype(jnp.bfloat16)
    for a, b in strips_of(rows):
        pick = (
            lax.broadcasted_iota(jnp.int32, (rows, b - a), 0) == line[:, a:b]
        ).astype(jnp.bfloat16)
        found = dot(table[...], pick, PLAIN)
        hot[a:b, :] = found.T.astype(jnp.bfloat16)
        damp[:, a:b] = jnp.sum(found[ntx + nrx :, :], axis=0, keepdims=True)


def rest_body(depth, strips, sens, *refs):
    for s, (a, b) in enumerate(strips):
        refs[len(strips) + s][...] = refs[s][...] + dot(sens[a:, :], sens[a:b, :], ROWS_ROWS)


def gram_body(ntx, nrx, count, stacked, first, some, hot, layer_cond, *refs):
    held = 1 if stacked else count
    blocks, refs = refs[:held], refs[held:]
    rows = hot.shape[0]
    bands = strips_of(rows)
    strips = bands[:some]
    before = () if first else refs[: len(strips)]
    after = refs[len(before) : len(before) + len(strips)]
    sens, conds = refs[-2:]
    nlayer = layer_cond.shape[0]
    size = blocks[0].shape[-1]

    def conductivities(cells, at):
        layer = cells[ntx + nrx : ntx + nrx + 1, :].astype(jnp.float32)
        level = lax.broadcasted_iota(jnp.int32, (nlayer, size), 0).astype(jnp.float32)
        cond = jnp.sum(jnp.where(level == layer, layer_cond[:, :1], 0.0), axis=0, keepdims=True)
        conds[at // size] = cond

    def fill(group):
        part = rows // PARTS

        def some(i, carry):
            here = pl.ds(pl.multiple_of(i * part, 16), part)
            for g, cells in enumerate(group):
                tx = dot(hot[here, :ntx], cells[:ntx, :], PLAIN)
                rx = dot(hot[here, ntx : ntx + nrx], cells[ntx : ntx + nrx, :], PLAIN)
                sens[here, g * size : (g + 1) * size] = (tx * rx * conds[g]).astype(jnp.bfloat16)
            return carry

        lax.fori_loop(0, PARTS, some, 0)

    def add(source, depth):
        for s, (a, b) in enumerate(strips):
            part = dot(sens[a:, :depth], sens[a:b, :depth], ROWS_ROWS)
            after[s][...] = part if source is None else source[s][...] + part

    if stacked:
        for s in range(len(strips)):
            after[s][...] = jnp.zeros_like(after[s]) if first else before[s][...]

        def one(i, carry):
            conductivities(blocks[0].at[i], 0)
            fill([blocks[0].at[i]])
            add(after, size)
            return carry

        lax.fori_loop(0, count, one, 0)
        return
    source = None if first else before
    for start in range(0, count, GROUP):
        group = blocks[start : start + GROUP]
        for i, cells in enumerate(group):
            conductivities(cells, i * size)
        fill(group)
        add(source, len(group) * size)
        source = after


class Panels:
    def __init__(self, pairs):
        self.pairs = pairs

    def of(self, k, a, b):
        s, c = divmod(k * BLOCK, STRIP)
        part = (slice(a - s * STRIP, b - s * STRIP), slice(c, c + BLOCK))
        return tuple(ref.at[part] for ref in self.pairs[s])

    def put(self, k, a, b, pair):
        for ref, value in zip(self.of(k, a, b), pair):
            ref[...] = value

    def sums(self, a, b, c, d, count):
        total = None
        for start in range(0, count * BLOCK, STRIP):
            s, width = start // STRIP, min(STRIP, count * BLOCK - start)
            high, low = self.pairs[s]
            base = s * STRIP
            left = tuple(ref[a - base : b - base, :width] for ref in (high, low))
            right = tuple(ref[c - base : d - base, :width] for ref in (high, low))
            part = product(left, right, ROWS_ROWS)
            total = part if total is None else total + part
        return total


def tiles_of(a, b, size=2 * BLOCK):
    return [(r, min(r + size, b)) for r in range(a, b, size)]


def factor_columns(first, last, rows, scale, mine, theirs, damping, panels, state, extra):
    column, corner, inverse, work, upper = state
    row = lax.broadcasted_iota(jnp.int32, (BLOCK, BLOCK), 0)
    col = lax.broadcasted_iota(jnp.int32, (BLOCK, BLOCK), 1)

    def gram(k, a, b):
        s, c = divmod(k * BLOCK, STRIP)
        part = (slice(a - s * STRIP, b - s * STRIP), slice(c, c + BLOCK))
        s -= first * BLOCK // STRIP
        value = (mine[s][part] + theirs[s][part]) * scale
        if a == k * BLOCK:
            ids = lax.broadcasted_iota(jnp.int32, (b - a, BLOCK), 0)
            across = lax.broadcasted_iota(jnp.int32, (b - a, BLOCK), 1)
            value = value + jnp.where(ids == across, damping[:, a : a + BLOCK], 0.0)
        return value

    def below(k, a, b):
        pair = (inverse[k % 2, 0], inverse[k % 2, 1])
        panels.put(k, a, b, halves(product(halves(column[k % 2, a:b, :]), pair, ROWS_ROWS)))

    def fill(k, a, b, count):
        value = gram(k, a, b)
        if count:
            value = value - panels.sums(a, b, k * BLOCK, (k + 1) * BLOCK, count)
        return value

    def fill_column(k, a, b):
        column[k % 2, a:b, :] = fill(k, a, b, k)

    def fill_corner(k):
        corner[...] = fill(k, k * BLOCK, (k + 1) * BLOCK, k - 1)

    diagonal = fill(first, first * BLOCK, (first + 1) * BLOCK, first)
    for k in range(first, last):
        at, end = k * BLOCK, (k + 1) * BLOCK
        calls = []
        for a, b in tiles_of(end, rows):
            if k > first:
                calls.append(functools.partial(below, k - 1, a, b))
            calls.append(functools.partial(fill_column, k, a, b))
        if k + 1 < last:
            calls.insert(min(2, len(calls)), functools.partial(fill_corner, k + 1))
        factor_block(diagonal, work, upper, calls + extra(k))
        pair = halves(upper[:, BLOCK:])
        inverse[k % 2, 0] = pair[0]
        inverse[k % 2, 1] = pair[1]
        if k + 1 < last:
            beneath = halves(product(halves(column[k % 2, end : end + BLOCK, :]), pair, ROWS_ROWS))
            diagonal = corner[...] - product(beneath, beneath, ROWS_ROWS)
            panels.put(k, end, end + BLOCK, beneath)
        panels.put(k, at, end, halves(jnp.where(row >= col, upper[:, :BLOCK].T, 0.0)))
        above = at - at % STRIP
        if above < at:
            zero = jnp.zeros((at - above, BLOCK), jnp.bfloat16)
            panels.put(k, above, at, (zero, zero))
    for a, b in tiles_of(last * BLOCK, rows):
        below(last - 1, a, b)


def start_body(cell_total, damping, mine, theirs, high, low, *state):
    factor_columns(
        0, STRIP // BLOCK, high.shape[0], 1.0 / cell_total, [mine], [theirs], damping,
        Panels([(high, low)]), state, lambda k: [],
    )


def finish_body(chosen_cols, cell_total, count, place, damping, order, high, low, *refs):
    mine, refs = refs[:count], refs[count:]
    theirs, refs = refs[:count], refs[count:]
    trailing, factor, refs = refs[0], refs[1], refs[2:]
    state, row_hot, pairs = refs[:5], refs[5], refs[6:]
    rows = order.shape[1]
    scale = 1.0 / cell_total
    pairs = [(high, low)] + list(zip(pairs[::2], pairs[1::2]))
    tile_cols, group_rows = trailing.shape

    def place_rows():
        row_hot[...] = (
            place[0] + lax.broadcasted_iota(jnp.int32, (group_rows, rows), 0) == order[...]
        ).astype(jnp.bfloat16)
        trailing[...] = jnp.zeros_like(trailing)

    def col_hot(a, b):
        return (
            place[1] + lax.broadcasted_iota(jnp.int32, (tile_cols, b - a), 0) == order[:, a:b]
        ).astype(jnp.bfloat16)

    def emit(s):
        at, end = s * STRIP, (s + 1) * STRIP
        high, low = pairs[s]
        rows_high = dot(row_hot[:, at:], high[...], PLAIN)
        rows_low = dot(row_hot[:, at:], low[...], PLAIN)
        factor[:, at:end] = rows_high + rows_low
        kept = jnp.sum(row_hot[:, chosen_cols:].astype(jnp.float32), axis=1, keepdims=True)
        picks = col_hot(chosen_cols, rows)
        cols_high = dot(picks, high[chosen_cols - at :, :], PLAIN)
        cols_low = dot(picks, low[chosen_cols - at :, :], PLAIN)
        trailing[...] -= product(
            (cols_high.astype(jnp.bfloat16), cols_low.astype(jnp.bfloat16)),
            ((rows_high * kept).astype(jnp.bfloat16), (rows_low * kept).astype(jnp.bfloat16)),
            ROWS_ROWS,
        )

    def remain(at, end):
        ids = lax.broadcasted_iota(jnp.int32, (rows - at, end - at), 0)
        across = lax.broadcasted_iota(jnp.int32, (rows - at, end - at), 1)
        s = at // STRIP - 1
        strip = (mine[s][...] + theirs[s][...]) * scale
        strip = strip + jnp.where(ids == across, damping[:, at:end], 0.0)
        for value in halves(strip):
            some = dot(row_hot[:, at:], value, PLAIN).astype(jnp.bfloat16)
            trailing[...] += dot(col_hot(at, end), some, ROWS_ROWS)
            if end < rows:
                some = dot(row_hot[:, at:end], value[end - at :, :], ROWS_ROWS).astype(jnp.bfloat16)
                trailing[...] += dot(col_hot(end, rows), some, ROWS_ROWS)

    last = chosen_cols // BLOCK
    per = STRIP // BLOCK
    calls = {k: [] for k in range(per, last)}
    calls[per].append(place_rows)
    for s in range(len(pairs) - 1):
        calls[min((s + 1) * per + 1, last - 1)].append(functools.partial(emit, s))
    for i, (at, end) in enumerate((a, b) for a, b in strips_of(rows) if a >= chosen_cols):
        calls[max(per + 1, last - 1 - i % 2 * per)].append(functools.partial(remain, at, end))
    factor_columns(
        per, last, rows, scale, mine, theirs, damping, Panels(pairs), state, lambda k: calls[k]
    )
    emit(len(pairs) - 1)


def shards(
    tx_fields, rx_fields, layer_of_cell, layer_cond, tx_of_row, rx_of_row, damping, panel_order
):
    grp_count = lax.axis_size("grp")
    tile_count = lax.axis_size("tile")
    tile_cells = tx_fields.shape[1]
    ntx, nrx = tx_fields.shape[0], rx_fields.shape[0]
    rows = tx_of_row.shape[0]
    group_rows = rows // grp_count
    tile_cols = rows // tile_count
    chosen_cols = PANEL * NPAN
    grp, tile = lax.axis_index("grp"), lax.axis_index("tile")

    half = tile_cells // 2
    start = (grp % 2) * half

    def piece(x):
        return lax.dynamic_slice_in_dim(x, start, half, axis=x.ndim - 1)

    own = jnp.concatenate(
        [
            piece(tx_fields),
            piece(rx_fields),
            jnp.broadcast_to(piece(layer_of_cell).astype(jnp.bfloat16)[None, :], (PAD, half)),
        ],
        axis=0,
    )

    inner = 1
    while inner * inner * 4 <= tile_count:
        inner *= 2
    outer = tile_count // inner

    def along(value, step):
        pairs = []
        for i in range(tile_count):
            o, n = divmod(i, inner)
            o = o ^ step[0] if outer & (outer - 1) == 0 else (o + step[0]) % outer
            n = n ^ step[1] if inner & (inner - 1) == 0 else (n + step[1]) % inner
            pairs.append((i, o * inner + n))
        return lax.ppermute(value, "tile", pairs)

    near = [along(own, (0, k)) for k in range(1, inner)]
    far = [along(own, (k, 0)) for k in range(1, outer)]
    relayed = [[along(far[0], (0, k)) for k in range(1, inner)]]

    width = -(-(ntx + nrx + 3) // BLOCK) * BLOCK
    hot, damp, order = pl.pallas_call(
        functools.partial(select_body, ntx, nrx),
        in_specs=[VMEM] * 4,
        out_specs=[VMEM] * 3,
        out_shape=[
            jax.ShapeDtypeStruct((rows, width), jnp.bfloat16),
            jax.ShapeDtypeStruct((1, rows), jnp.float32),
            jax.ShapeDtypeStruct((1, rows), jnp.int32),
        ],
        scratch_shapes=[pltpu.VMEM((width, rows), jnp.bfloat16)],
        compiler_params=pltpu.CompilerParams(
            vmem_limit_bytes=grant(((rows, width), 8), ((rows, STRIP), 8))
        ),
        cost_estimate=pl.CostEstimate(
            flops=2 * width * rows * rows, bytes_accessed=4 * rows * width, transcendentals=0
        ),
    )(panel_order, tx_of_row, rx_of_row, damping)

    strips = strips_of(rows)
    strip_shapes = [jax.ShapeDtypeStruct((rows - a, b - a), jnp.float32) for a, b in strips]
    lower = sum((rows - a) * (b - a) for a, b in strips)
    conds = jnp.broadcast_to(layer_cond[:, None], (layer_cond.shape[0], BLOCK))

    def swap(value):
        return lax.ppermute(value, "grp", [(i, i ^ 1) for i in range(grp_count)])

    def add(blocks, sums, some=None):
        count = len(blocks)
        stacked = count > GROUP
        depth = half * (1 if stacked else min(count, GROUP))
        args = [jnp.stack(blocks)] if stacked else blocks
        chosen = strips[:some]
        cost = 2 * count * half * (sum((rows - a) * (b - a) for a, b in chosen) + rows * STRIP * 2)
        sens = jax.ShapeDtypeStruct((rows, depth), jnp.bfloat16)
        kept = some is not None
        return pl.pallas_call(
            functools.partial(gram_body, ntx, nrx, count, stacked, not sums, some),
            in_specs=[VMEM] * (2 + len(args) + len(sums[:some])),
            out_specs=[VMEM] * (len(chosen) + kept),
            out_shape=strip_shapes[:some] + [sens] * kept,
            scratch_shapes=([] if kept else [pltpu.VMEM(sens.shape, sens.dtype)])
            + [pltpu.VMEM((GROUP, 1, half), jnp.float32)],
            input_output_aliases={2 + len(args) + i: i for i in range(len(sums[:some]))},
            compiler_params=pltpu.CompilerParams(
                vmem_limit_bytes=grant(
                    ((lower,), 8), ((rows, depth), 2), ((rows, width), 2), ((count, own.size), 2)
                )
            ),
            cost_estimate=pl.CostEstimate(
                flops=cost, bytes_accessed=8 * lower, transcendentals=0
            ),
        )(hot, conds, *args, *sums[:some])

    sums = list(add([own] + near + far[:1], []))
    held = lax.optimization_barrier((tuple(far[1:]), tuple(sums)))
    far, sums = far[:1] + list(held[0]), list(held[1])
    relayed += [[along(value, (0, k)) for k in range(1, inner)] for value in far[1:]]
    sums = list(add(far[1:] + relayed[0], sums))
    blocks = [value for values in relayed[1:] for value in values]
    if len(blocks) > GROUP:
        sums = list(add(blocks, sums))
        theirs = [swap(sums[0])]
    else:
        one, sens = add(blocks, sums, 1)
        theirs = [swap(one)]
        others = strips[1:]
        sums = [one] + list(
            pl.pallas_call(
                functools.partial(rest_body, sens.shape[1], others),
                in_specs=[VMEM] * (1 + len(others)),
                out_specs=[VMEM] * len(others),
                out_shape=strip_shapes[1:],
                input_output_aliases={1 + i: i for i in range(len(others))},
                compiler_params=pltpu.CompilerParams(
                    vmem_limit_bytes=grant(((lower,), 8), (sens.shape, 2))
                ),
                cost_estimate=pl.CostEstimate(
                    flops=2 * lower * sens.shape[1], bytes_accessed=8 * lower, transcendentals=0
                ),
            )(sens, *sums[1:])
        )
    theirs += [swap(value) for value in sums[1:]]

    state = [
        pltpu.VMEM((2, rows, BLOCK), jnp.float32),
        pltpu.VMEM((BLOCK, BLOCK), jnp.float32),
        pltpu.VMEM((2, 2, BLOCK, BLOCK), jnp.bfloat16),
        pltpu.VMEM((BLOCK, 2 * BLOCK), jnp.float32),
        pltpu.VMEM((BLOCK, 2 * BLOCK), jnp.float32),
    ]
    cell_total = tile_cells * tile_count
    high, low = pl.pallas_call(
        functools.partial(start_body, cell_total),
        in_specs=[VMEM] * 3,
        out_specs=[VMEM] * 2,
        out_shape=[jax.ShapeDtypeStruct((rows, STRIP), jnp.bfloat16)] * 2,
        scratch_shapes=state,
        compiler_params=pltpu.CompilerParams(
            vmem_limit_bytes=grant(((rows, STRIP), 12), ((rows, BLOCK), 8), ((rows, STRIP), 8))
        ),
        cost_estimate=pl.CostEstimate(
            flops=rows * STRIP * cell_total, bytes_accessed=8 * rows * STRIP, transcendentals=0
        ),
    )(damp, sums[0], theirs[0])

    place = jnp.stack([grp * group_rows, tile * tile_cols]).astype(jnp.int32)
    later = [(rows - a, STRIP) for a in range(STRIP, chosen_cols, STRIP)]
    trailing, factor = (
        pl.pallas_call(
            functools.partial(finish_body, chosen_cols, cell_total, len(strips) - 1),
            in_specs=[SMEM] + [VMEM] * (2 + 2 * len(strips)),
            out_specs=[VMEM, VMEM],
            out_shape=[
                jax.ShapeDtypeStruct((tile_cols, group_rows), jnp.float32),
                jax.ShapeDtypeStruct((group_rows, chosen_cols), jnp.float32),
            ],
            scratch_shapes=state
            + [pltpu.VMEM((group_rows, rows), jnp.bfloat16)]
            + [pltpu.VMEM(shape, jnp.bfloat16) for shape in later for _ in range(2)],
            compiler_params=pltpu.CompilerParams(
                vmem_limit_bytes=grant(
                    ((lower,), 8), ((rows, chosen_cols), 4), ((rows, BLOCK), 16),
                    ((group_rows, chosen_cols + STRIP), 4), ((group_rows, rows), 4),
                )
            ),
            cost_estimate=pl.CostEstimate(
                flops=6 * rows * rows * chosen_cols, bytes_accessed=8 * lower, transcendentals=0
            ),
        )(place, damp, order, high, low, *sums[1:], *theirs[1:])
    )
    return trailing.T, factor


def solution(mesh):
    placed = (P(None, "tile"), P(None, "tile"), P("tile"), P(), P(), P(), P(), P())
    return jax.shard_map(
        shards,
        mesh=mesh,
        in_specs=placed,
        out_specs=(P("grp", "tile"), P("grp", None)),
        check_vma=False,
    )
```

profile of v0, /device:TPU:0, one launch (start us, length us, event | category | flops | bytes accessed | tf_op | source)
XLA Modules:
  0.0 83.1 jit_solution(8601219704175249720)
XLA Ops:
  0.6 0.0 copy-start
  0.7 0.8 dynamic-slice_convert_fusion
  1.5 0.8 %constant_dynamic-slice_fusion.1 = bf16[64,512]{1,0:T(8,128)(2,1)S(1)} fusion(bf16[64,1024]{1,0:T(8,128)(2,1)} %param.8, s32[]{:T(128)S(6)} %select_n.13), kind=kLoop, calls=%fused_computation.4 | loop fusion | bytes 131076 | tf_op jit(solution)/shard_map/dynamic_slice | solution.py:373
  2.3 0.0 copy-done
  2.3 0.0 copy-start.7
  2.4 3.1 %collective-permute-start.3 = (bf16[208,512]{1,0:T(8,128)(2,1)S(1)}, bf16[208,512]{1,0:T(8,128)(2,1)S(1)}, u32[]{:S(2)}, u32[]{:S(2)}) collective-permute-start(bf16[208,512]{1,0:T(8,128)(2,1)S(1)} %pad_maximum_fusion.refs_0_), channel_id=1, source_target_pairs={{0,2},{1,3},{2,0},{3,1},{4,6},{5,7},{6,4},{7,5},{8,10},{9,11},{10,... | collective-permute-start | bytes 638984 | tf_op jit(solution)/shard_map/ppermute | solution.py:396
  5.5 1.5 %collective-permute-start.2 = (bf16[208,512]{1,0:T(8,128)(2,1)S(1)}, bf16[208,512]{1,0:T(8,128)(2,1)S(1)}, u32[]{:S(2)}, u32[]{:S(2)}) collective-permute-start(bf16[208,512]{1,0:T(8,128)(2,1)S(1)} %pad_maximum_fusion.refs_0_), channel_id=1, source_target_pairs={{0,1},{1,0},{2,3},{3,2},{4,5},{5,4},{6,7},{7,6},{8,9},{9,8},{10,11... | collective-permute-start | bytes 638984 | tf_op jit(solution)/shard_map/ppermute | solution.py:396
  7.0 2.5 %collective-permute-start.1 = (bf16[208,512]{1,0:T(8,128)(2,1)S(1)}, bf16[208,512]{1,0:T(8,128)(2,1)S(1)}, u32[]{:S(2)}, u32[]{:S(2)}) collective-permute-start(bf16[208,512]{1,0:T(8,128)(2,1)S(1)} %pad_maximum_fusion.refs_0_), channel_id=1, source_target_pairs={{0,6},{1,7},{2,4},{3,5},{4,2},{5,3},{6,0},{7,1},{8,14},{9,15},{10,... | collective-permute-start | bytes 638984 | tf_op jit(solution)/shard_map/ppermute | solution.py:396
  9.5 0.1 collective-permute-start
  9.6 0.0 copy-start.3
  9.6 0.7 copy-done.3
  10.3 0.0 copy-start.4
  10.3 0.7 copy-done.4
  11.0 0.0 copy-start.5
  11.0 0.7 copy-done.5
  11.7 0.0 copy-start.6
  11.7 0.7 copy-done.6
  12.4 1.7 %shard_map.95 = (bf16[1408,256]{1,0:T(8,128)(2,1)S(1)}, f32[1,1408]{1,0:T(1,128)S(1)}, s32[1,1408]{1,0:T(1,128)S(1)}) custom-call(s32[1408]{0:T(1024)S(1)} %copy-done.3, s32[1408]{0:T(1024)S(1)} %copy-done.4, s32[1408]{0:T(1024)S(1)} %copy-done.5, f32[1408]{0:T(1024)S(1)} %copy-done.6), custom_call_target="tpu_custom_call" | custom-call | flops 1015021568 | bytes 1441792 | tf_op jit(solution)/shard_map/pallas_call | solution.py:403
  14.0 0.0 collective-permute-done.3.refs_2_
  14.0 0.6 collective-permute-start.6
  14.6 0.0 collective-permute-done.2.refs_1_
  14.6 0.0 copy-done.7
  14.6 0.1 broadcast_in_dim.4.layer_cond
  14.7 7.9 %shard_map.96 = (f32[1408,256]{1,0:T(8,128)S(1)}, f32[1152,256]{1,0:T(8,128)}, f32[896,256]{1,0:T(8,128)}, f32[640,256]{1,0:T(8,128)}, f32[384,256]{1,0:T(8,128)}, /*index=5*/f32[128,128]{1,0:T(8,128)S(1)}) custom-call(bf16[1408,256]{1,0:T(8,128)(2,1)S(1)} %get-tuple-element.38.hot, f32[32,128]{1,0:T(8,128)S(1)} %broadcast_in_dim.4.layer_cond, ...), custom_call_target="tpu_custom_call" | custom-call | flops 5788139520 | bytes 9306112 | tf_op jit(solution)/shard_map/pallas_call | solution.py:438
  22.6 0.0 collective-permute-done.1.refs_1_
  22.6 5.4 %collective-permute-done.refs_0_ = bf16[208,512]{1,0:T(8,128)(2,1)S(1)} collective-permute-done((bf16[208,512]{1,0:T(8,128)(2,1)S(1)}, bf16[208,512]{1,0:T(8,128)(2,1)S(1)}, u32[]{:S(2)}, u32[]{:S(2)}) %collective-permute-start) | collective-permute-done | bytes 213024 | tf_op jit(solution)/shard_map/ppermute | solution.py:396
  28.0 0.5 collective-permute-start.4
  28.5 1.5 %collective-permute-start.5 = (bf16[208,512]{1,0:T(8,128)(2,1)S(1)}, bf16[208,512]{1,0:T(8,128)(2,1)S(1)}, u32[]{:S(2)}, u32[]{:S(2)}) collective-permute-start(bf16[208,512]{1,0:T(8,128)(2,1)S(1)} %collective-permute-done.1.refs_1_), channel_id=1, source_target_pairs={{0,1},{1,0},{2,3},{3,2},{4,5},{5,4},{6,7},{7,6},{8,9},{9,8},{10,11... | collective-permute-start | bytes 638984 | tf_op jit(solution)/shard_map/ppermute | solution.py:396
  30.0 0.0 collective-permute-done.6.refs_2_
  30.0 9.8 %shard_map.97 = (f32[1408,256]{1,0:T(8,128)S(1)}, f32[1152,256]{1,0:T(8,128)}, f32[896,256]{1,0:T(8,128)}, f32[640,256]{1,0:T(8,128)}, f32[384,256]{1,0:T(8,128)}, /*index=5*/f32[128,128]{1,0:T(8,128)S(1)}) custom-call(bf16[1408,256]{1,0:T(8,128)(2,1)S(1)} %get-tuple-element.38.hot, ...), custom_call_target="tpu_custom_call", output_to_operand_aliasing={{0}: (5, {}), {1}: (6, {}), {2}: (7, {}), {3}: (8, {}), {4}... | custom-call | flops 5788139520 | bytes 9306112 | tf_op jit(solution)/shard_map/pallas_call | solution.py:438
  39.8 0.0 collective-permute-done.4.refs_0_
  39.8 0.0 collective-permute-done.5.refs_1_
  39.8 3.4 %shard_map.98 = (f32[1408,256]{1,0:T(8,128)S(1)}, bf16[1408,1024]{1,0:T(8,128)(2,1)S(1)}) custom-call(bf16[1408,256]{1,0:T(8,128)(2,1)S(1)} %get-tuple-element.38.hot, f32[32,128]{1,0:T(8,128)S(1)} %broadcast_in_dim.4.layer_cond, bf16[208,512]{1,0:T(8,128)(2,1)S(1)} %collective-permute-done.4.refs_0_, ...), custom_call_target="tpu_custom_call", output_to_operand_aliasing={{0}: (4, {})} | custom-call | flops 2214592512 | bytes 9306112 | tf_op jit(solution)/shard_map/pallas_call | solution.py:438
  43.2 0.1 collective-permute-start.7
  43.3 4.9 %shard_map.100 = (f32[1152,256]{1,0:T(8,128)}, f32[896,256]{1,0:T(8,128)}, f32[640,256]{1,0:T(8,128)}, f32[384,256]{1,0:T(8,128)}, f32[128,128]{1,0:T(8,128)S(1)}) custom-call(bf16[1408,1024]{1,0:T(8,128)(2,1)S(1)} %get-tuple-element.57.sens, ...), custom_call_target="tpu_custom_call", output_to_operand_aliasing={{0}: (1, {}), {1}: (2, {}), {2}: (3, {}), {3}: (4, {}), {4}... | custom-call | flops 2382364672 | bytes 9306112 | tf_op jit(solution)/shard_map/pallas_call | solution.py:470
  48.2 0.0 copy-start.1
  48.2 0.6 copy-done.1
  48.9 0.5 collective-permute-start.8
  49.3 0.0 collective-permute-start.9
  49.4 0.5 collective-permute-start.10
  49.9 0.0 collective-permute-start.11
  49.9 0.1 pad_add_fusion.place
  50.0 0.0 collective-permute-done.7.theirs
  50.0 0.5 collective-permute-start.12
  50.4 0.0 copy-start.2
  50.5 6.2 %shard_map.99 = (bf16[1408,256]{1,0:T(8,128)(2,1)S(1)}, bf16[1408,256]{1,0:T(8,128)(2,1)S(1)}) custom-call(f32[1,1408]{1,0:T(1,128)S(1)} %get-tuple-element.36.damping, f32[1408,256]{1,0:T(8,128)S(1)} %get-tuple-element.54.mine, f32[1408,256]{1,0:T(8,128)S(1)} %collective-permute-done.7.theirs), custom_call_target="tpu_custom_call" | custom-call | flops 2952790016 | bytes 2883584 | tf_op jit(solution)/shard_map/pallas_call | solution.py:494
  56.7 0.0 collective-permute-done.12.refs_9_
  56.7 0.0 collective-permute-done.11.refs_8_
  56.7 0.0 collective-permute-done.10.refs_7_
  56.7 0.0 collective-permute-done.9.refs_6_
  56.7 0.0 collective-permute-done.8.refs_5_
  56.7 0.0 copy-done.2
  56.8 26.4 %shard_map.101 = (f32[176,352]{1,0:T(8,128)}, f32[352,1024]{1,0:T(8,128)}) custom-call(s32[2]{0:T(128)S(1)} %pad_add_fusion.place, f32[1,1408]{1,0:T(1,128)S(1)} %get-tuple-element.36.damping, s32[1,1408]{1,0:T(1,128)S(1)} %get-tuple-element.37.order, bf16[1408,256]{1,0:T(8,128)(2,1)S(1)} %get-tuple-element.55.high, ...), custom_call_target="tpu_custom_call" | custom-call | flops 12180258816 | bytes 9306112 | tf_op jit(solution)/shard_map/pallas_call | solution.py:511
  (3 shorter events, 0.0 us)
Async XLA Ops:
  0.6 1.7 %copy-start = (bf16[128,1024]{1,0:T(8,128)(2,1)S(1)}, bf16[128,1024]{1,0:T(8,128)(2,1)}, u32[]{:S(2)}) copy-start(bf16[128,1024]{1,0:T(8,128)(2,1)} %param.9) | copy-start | bytes 786436
  2.3 12.3 %copy-start.7 = (f32[32]{0:T(128)S(1)}, f32[32]{0:T(128)}, u32[]{:S(2)}) copy-start(f32[32]{0:T(128)} %param.11) | copy-start | bytes 388
  2.4 11.7 %collective-permute-start.3 = (bf16[208,512]{1,0:T(8,128)(2,1)S(1)}, bf16[208,512]{1,0:T(8,128)(2,1)S(1)}, u32[]{:S(2)}, u32[]{:S(2)}) collective-permute-start(bf16[208,512]{1,0:T(8,128)(2,1)S(1)} %pad_maximum_fusion.refs_0_), channel_id=1, source_target_pairs={{0,2},{1,3},{2,0},{3,1},{4,6},{5,7},{6,4},{7,5},{8,10},{9,11},{10,... | collective-permute-start | bytes 638984 | tf_op jit(solution)/shard_map/ppermute | solution.py:396
  5.5 9.2 %collective-permute-start.2 = (bf16[208,512]{1,0:T(8,128)(2,1)S(1)}, bf16[208,512]{1,0:T(8,128)(2,1)S(1)}, u32[]{:S(2)}, u32[]{:S(2)}) collective-permute-start(bf16[208,512]{1,0:T(8,128)(2,1)S(1)} %pad_maximum_fusion.refs_0_), channel_id=1, source_target_pairs={{0,1},{1,0},{2,3},{3,2},{4,5},{5,4},{6,7},{7,6},{8,9},{9,8},{10,11... | collective-permute-start | bytes 638984 | tf_op jit(solution)/shard_map/ppermute | solution.py:396
  7.0 15.6 %collective-permute-start.1 = (bf16[208,512]{1,0:T(8,128)(2,1)S(1)}, bf16[208,512]{1,0:T(8,128)(2,1)S(1)}, u32[]{:S(2)}, u32[]{:S(2)}) collective-permute-start(bf16[208,512]{1,0:T(8,128)(2,1)S(1)} %pad_maximum_fusion.refs_0_), channel_id=1, source_target_pairs={{0,6},{1,7},{2,4},{3,5},{4,2},{5,3},{6,0},{7,1},{8,14},{9,15},{10,... | collective-permute-start | bytes 638984 | tf_op jit(solution)/shard_map/ppermute | solution.py:396
  9.5 18.5 %collective-permute-start = (bf16[208,512]{1,0:T(8,128)(2,1)S(1)}, bf16[208,512]{1,0:T(8,128)(2,1)S(1)}, u32[]{:S(2)}, u32[]{:S(2)}) collective-permute-start(bf16[208,512]{1,0:T(8,128)(2,1)S(1)} %pad_maximum_fusion.refs_0_), channel_id=1, source_target_pairs={{0,4},{1,5},{2,6},{3,7},{4,0},{5,1},{6,2},{7,3},{8,12},{9,13},{10,... | collective-permute-start | bytes 638984 | tf_op jit(solution)/shard_map/ppermute | solution.py:396
  9.6 0.7 copy-start.3
  10.3 0.7 copy-start.4
  11.0 0.7 copy-start.5
  11.7 0.7 copy-start.6
  14.0 15.9 %collective-permute-start.6 = (bf16[208,512]{1,0:T(8,128)(2,1)S(1)}, bf16[208,512]{1,0:T(8,128)(2,1)S(1)}, u32[]{:S(2)}, u32[]{:S(2)}) collective-permute-start(bf16[208,512]{1,0:T(8,128)(2,1)S(1)} %collective-permute-done.3.refs_2_), channel_id=1, source_target_pairs={{0,1},{1,0},{2,3},{3,2},{4,5},{5,4},{6,7},{7,6},{8,9},{9,8},{10,11... | collective-permute-start | bytes 638984 | tf_op jit(solution)/shard_map/ppermute | solution.py:396
  28.0 11.9 %collective-permute-start.4 = (bf16[208,512]{1,0:T(8,128)(2,1)S(1)}, bf16[208,512]{1,0:T(8,128)(2,1)S(1)}, u32[]{:S(2)}, u32[]{:S(2)}) collective-permute-start(bf16[208,512]{1,0:T(8,128)(2,1)S(1)} %collective-permute-done.refs_0_), channel_id=1, source_target_pairs={{0,1},{1,0},{2,3},{3,2},{4,5},{5,4},{6,7},{7,6},{8,9},{9,8},{10,11... | collective-permute-start | bytes 638984 | tf_op jit(solution)/shard_map/ppermute | solution.py:396
  28.5 11.4 %collective-permute-start.5 = (bf16[208,512]{1,0:T(8,128)(2,1)S(1)}, bf16[208,512]{1,0:T(8,128)(2,1)S(1)}, u32[]{:S(2)}, u32[]{:S(2)}) collective-permute-start(bf16[208,512]{1,0:T(8,128)(2,1)S(1)} %collective-permute-done.1.refs_1_), channel_id=1, source_target_pairs={{0,1},{1,0},{2,3},{3,2},{4,5},{5,4},{6,7},{7,6},{8,9},{9,8},{10,11... | collective-permute-start | bytes 638984 | tf_op jit(solution)/shard_map/ppermute | solution.py:396
  43.2 6.7 %collective-permute-start.7 = (f32[1408,256]{1,0:T(8,128)S(1)}, f32[1408,256]{1,0:T(8,128)S(1)}, u32[]{:S(2)}, u32[]{:S(2)}) collective-permute-start(f32[1408,256]{1,0:T(8,128)S(1)} %get-tuple-element.54.mine), channel_id=1, source_target_pairs={{0,8},{8,0},{16,24},{24,16},{1,9},{9,1},{17,25},{25,17},{2,10},{10... | collective-permute-start | bytes 4325384 | tf_op jit(solution)/shard_map/ppermute | solution.py:427
  48.2 0.6 copy-start.1
  48.9 7.9 %collective-permute-start.8 = (f32[1152,256]{1,0:T(8,128)}, f32[1152,256]{1,0:T(8,128)}, u32[]{:S(2)}, u32[]{:S(2)}) collective-permute-start(f32[1152,256]{1,0:T(8,128)} %get-tuple-element.63.refs_0_), channel_id=1, source_target_pairs={{0,8},{8,0},{16,24},{24,16},{1,9},{9,1},{17,25},{25,17},{2,10},{10... | collective-permute-start | bytes 3538952 | tf_op jit(solution)/shard_map/ppermute | solution.py:427
  49.3 7.4 %collective-permute-start.9 = (f32[896,256]{1,0:T(8,128)}, f32[896,256]{1,0:T(8,128)}, u32[]{:S(2)}, u32[]{:S(2)}) collective-permute-start(f32[896,256]{1,0:T(8,128)} %get-tuple-element.64.refs_1_), channel_id=1, source_target_pairs={{0,8},{8,0},{16,24},{24,16},{1,9},{9,1},{17,25},{25,17},{2,10},{10... | collective-permute-start | bytes 2752520 | tf_op jit(solution)/shard_map/ppermute | solution.py:427
  49.4 7.3 %collective-permute-start.10 = (f32[640,256]{1,0:T(8,128)}, f32[640,256]{1,0:T(8,128)}, u32[]{:S(2)}, u32[]{:S(2)}) collective-permute-start(f32[640,256]{1,0:T(8,128)} %get-tuple-element.65.refs_2_), channel_id=1, source_target_pairs={{0,8},{8,0},{16,24},{24,16},{1,9},{9,1},{17,25},{25,17},{2,10},{10... | collective-permute-start | bytes 1966088 | tf_op jit(solution)/shard_map/ppermute | solution.py:427
  49.9 6.8 %collective-permute-start.11 = (f32[384,256]{1,0:T(8,128)}, f32[384,256]{1,0:T(8,128)S(1)}, u32[]{:S(2)}, u32[]{:S(2)}) collective-permute-start(f32[384,256]{1,0:T(8,128)} %get-tuple-element.66.refs_3_), channel_id=1, source_target_pairs={{0,8},{8,0},{16,24},{24,16},{1,9},{9,1},{17,25},{25,17},{2,10},{10... | collective-permute-start | bytes 1179656 | tf_op jit(solution)/shard_map/ppermute | solution.py:427
  50.0 6.7 %collective-permute-start.12 = (f32[128,128]{1,0:T(8,128)}, f32[128,128]{1,0:T(8,128)S(1)}, u32[]{:S(2)}, u32[]{:S(2)}) collective-permute-start(f32[128,128]{1,0:T(8,128)} %copy-done.1), channel_id=1, source_target_pairs={{0,8},{8,0},{16,24},{24,16},{1,9},{9,1},{17,25},{25,17},{2,10},{10... | collective-permute-start | bytes 196616 | tf_op jit(solution)/shard_map/ppermute | solution.py:427
  50.4 6.3 %copy-start.2 = (f32[128,128]{1,0:T(8,128)S(1)}, f32[128,128]{1,0:T(8,128)}, u32[]{:S(2)}) copy-start(f32[128,128]{1,0:T(8,128)} %copy-done.1) | copy-start | bytes 196612
where the time goes:
time: 83.6 us; the launch traced here: 83.1 us
  Pallas kernels  60.3 us (72%)
  starting transfers between devices  11.4 us (14%)
  waiting for transfers between devices  5.41 us (6%)
  local copies, waits for them, and re-layouts  4.36 us (5%)
  other arithmetic  0.89 us (1%)
    pallas_call x1, Pallas kernels, shards(): pl.pallas_call(functools.partial(finish_body, chosen_cols, cell_total, le...  26.4 us
    pallas_call x3, Pallas kernels, add(): pl.pallas_call(functools.partial(gram_body, ntx, nrx, count, stacked, not...  21.1 us
    ppermute x7, starting transfers between devices, along(): return lax.ppermute(value, 'tile', pairs)  9.8 us
    pallas_call x1, Pallas kernels, shards(): pl.pallas_call(functools.partial(start_body, cell_total), in_specs=[VMEM]...  6.23 us
    ppermute x7, waiting for transfers between devices, along(): return lax.ppermute(value, 'tile', pairs)  5.39 us
    pallas_call x1, Pallas kernels, shards(): pl.pallas_call(functools.partial(rest_body, sens.shape[1], others), in_sp...  4.93 us
    unnamed x16, local copies, waits for them, and re-layouts  3.43 us
  transfers between devices with their start and end apart: 13, of which 1 were waited for; matrix products, arithmetic and copies ran while one was open for 0% of the time, Pallas kernels for 37%

commit v1 on v0

--- a/solution.py
+++ b/solution.py
@@ -102,8 +102,41 @@
     return [(a, min(a + STRIP, rows)) for a in range(0, rows, STRIP)]
 
 
-def select_body(ntx, nrx, order, tx_of_row, rx_of_row, damping, hot, damp, line, table):
+def own_body(tx_fields, rx_fields, layer_of_cell, out, layer, sems):
+    ntx, nrx, half = tx_fields.shape[0], rx_fields.shape[0], out.shape[1]
+    start = pl.multiple_of(lax.rem(lax.axis_index("grp"), 2) * half, half)
+    copies = [
+        pltpu.make_async_copy(layer_of_cell.at[pl.ds(start, half)], layer, sems.at[0]),
+        pltpu.make_async_copy(tx_fields.at[:, pl.ds(start, half)], out.at[:ntx], sems.at[1]),
+        pltpu.make_async_copy(
+            rx_fields.at[:, pl.ds(start, half)], out.at[ntx : ntx + nrx], sems.at[2]
+        ),
+    ]
+    for copy in copies:
+        copy.start()
+    copies[0].wait()
+    line = layer[...].reshape(1, half).astype(jnp.float32)
+    out[ntx + nrx :, :] = jnp.broadcast_to(line, (PAD, half)).astype(jnp.bfloat16)
+    for copy in copies[1:]:
+        copy.wait()
+
+
+def select_body(
+    ntx, nrx, order, tx_of_row, rx_of_row, damping, own, layer_cond, hot, damp, line, sens, table, ints, floats, sems
+):
     rows = order.shape[0]
+    copies = [
+        pltpu.make_async_copy(source, target, sems.at[i])
+        for i, (source, target) in enumerate(
+            zip((order, tx_of_row, rx_of_row, damping), list(ints) + [floats])
+        )
+    ]
+    for copy in copies:
+        copy.start()
+    for copy in copies:
+        copy.wait()
+    order, tx_of_row, rx_of_row = ints
+    damping = floats
     table[:ntx, :] = (
         lax.broadcasted_iota(jnp.int32, (ntx, rows), 0) == tx_of_row[...].reshape(1, rows)
     ).astype(jnp.bfloat16)
@@ -128,6 +161,30 @@
         found = dot(table[...], pick, PLAIN)
         hot[a:b, :] = found.T.astype(jnp.bfloat16)
         damp[:, a:b] = jnp.sum(found[ntx + nrx :, :], axis=0, keepdims=True)
+    sensitivities(ntx, nrx, [own], [conductivities(ntx, nrx, own, layer_cond)], hot, sens)
+
+
+def conductivities(ntx, nrx, cells, layer_cond):
+    nlayer, size = layer_cond.shape[0], cells.shape[-1]
+    layer = cells[ntx + nrx : ntx + nrx + 1, :].astype(jnp.float32)
+    level = lax.broadcasted_iota(jnp.int32, (nlayer, size), 0).astype(jnp.float32)
+    return jnp.sum(jnp.where(level == layer, layer_cond[:, :1], 0.0), axis=0, keepdims=True)
+
+
+def sensitivities(ntx, nrx, group, conds, hot, sens, at=0):
+    rows = hot.shape[0]
+    part = rows // PARTS
+
+    def some(i, carry):
+        here = pl.ds(pl.multiple_of(i * part, 16), part)
+        for g, cells in enumerate(group):
+            size = cells.shape[-1]
+            tx = dot(hot[here, :ntx], cells[:ntx, :], PLAIN)
+            rx = dot(hot[here, ntx : ntx + nrx], cells[ntx : ntx + nrx, :], PLAIN)
+            sens[here, at + g * size : at + (g + 1) * size] = (tx * rx * conds[g][...]).astype(jnp.bfloat16)
+        return carry
+
+    lax.fori_loop(0, PARTS, some, 0)
 
 
 def rest_body(depth, strips, sens, *refs):
@@ -136,35 +193,19 @@
 
 
 def gram_body(ntx, nrx, count, stacked, first, some, hot, layer_cond, *refs):
-    held = 1 if stacked else count
+    held = 1 + first if stacked else count
     blocks, refs = refs[:held], refs[held:]
     rows = hot.shape[0]
-    bands = strips_of(rows)
-    strips = bands[:some]
+    strips = strips_of(rows)[:some]
     before = () if first else refs[: len(strips)]
     after = refs[len(before) : len(before) + len(strips)]
     sens, conds = refs[-2:]
-    nlayer = layer_cond.shape[0]
-    size = blocks[0].shape[-1]
-
-    def conductivities(cells, at):
-        layer = cells[ntx + nrx : ntx + nrx + 1, :].astype(jnp.float32)
-        level = lax.broadcasted_iota(jnp.int32, (nlayer, size), 0).astype(jnp.float32)
-        cond = jnp.sum(jnp.where(level == layer, layer_cond[:, :1], 0.0), axis=0, keepdims=True)
-        conds[at // size] = cond
-
-    def fill(group):
-        part = rows // PARTS
-
-        def some(i, carry):
-            here = pl.ds(pl.multiple_of(i * part, 16), part)
-            for g, cells in enumerate(group):
-                tx = dot(hot[here, :ntx], cells[:ntx, :], PLAIN)
-                rx = dot(hot[here, ntx : ntx + nrx], cells[ntx : ntx + nrx, :], PLAIN)
-                sens[here, g * size : (g + 1) * size] = (tx * rx * conds[g]).astype(jnp.bfloat16)
-            return carry
-
-        lax.fori_loop(0, PARTS, some, 0)
+    size = blocks[-1].shape[-1]
+
+    def fill(group, at=0):
+        for g, cells in enumerate(group):
+            conds[g] = conductivities(ntx, nrx, cells, layer_cond)
+        sensitivities(ntx, nrx, group, [conds.at[g] for g in range(len(group))], hot, sens, at)
 
     def add(source, depth):
         for s, (a, b) in enumerate(strips):
@@ -172,25 +213,24 @@
             after[s][...] = part if source is None else source[s][...] + part
 
     if stacked:
-        for s in range(len(strips)):
-            after[s][...] = jnp.zeros_like(after[s]) if first else before[s][...]
+        if first:
+            sens[...] = blocks[0][...]
+            add(None, size)
+        else:
+            for s in range(len(strips)):
+                after[s][...] = before[s][...]
 
         def one(i, carry):
-            conductivities(blocks[0].at[i], 0)
-            fill([blocks[0].at[i]])
+            fill([blocks[-1].at[i]])
             add(after, size)
             return carry
 
-        lax.fori_loop(0, count, one, 0)
+        lax.fori_loop(0, count - first, one, 0)
         return
-    source = None if first else before
-    for start in range(0, count, GROUP):
-        group = blocks[start : start + GROUP]
-        for i, cells in enumerate(group):
-            conductivities(cells, i * size)
-        fill(group)
-        add(source, len(group) * size)
-        source = after
+    if first:
+        sens[:, :size] = blocks[0][...]
+    fill(blocks[first:], size if first else 0)
+    add(None if first else before, count * size)
 
 
 class Panels:
@@ -367,19 +407,14 @@
     grp, tile = lax.axis_index("grp"), lax.axis_index("tile")
 
     half = tile_cells // 2
-    start = (grp % 2) * half
-
-    def piece(x):
-        return lax.dynamic_slice_in_dim(x, start, half, axis=x.ndim - 1)
-
-    own = jnp.concatenate(
-        [
-            piece(tx_fields),
-            piece(rx_fields),
-            jnp.broadcast_to(piece(layer_of_cell).astype(jnp.bfloat16)[None, :], (PAD, half)),
-        ],
-        axis=0,
-    )
+    own = pl.pallas_call(
+        own_body,
+        in_specs=[pl.BlockSpec(memory_space=pl.ANY)] * 3,
+        out_specs=VMEM,
+        out_shape=jax.ShapeDtypeStruct((ntx + nrx + PAD, half), jnp.bfloat16),
+        scratch_shapes=[pltpu.VMEM((half,), jnp.int32), pltpu.SemaphoreType.DMA((3,))],
+        compiler_params=pltpu.CompilerParams(vmem_limit_bytes=grant()),
+    )(tx_fields, rx_fields, layer_of_cell)
 
     inner = 1
     while inner * inner * 4 <= tile_count:
@@ -400,28 +435,34 @@
     relayed = [[along(far[0], (0, k)) for k in range(1, inner)]]
 
     width = -(-(ntx + nrx + 3) // BLOCK) * BLOCK
-    hot, damp, order = pl.pallas_call(
+    conds = jnp.broadcast_to(layer_cond[:, None], (layer_cond.shape[0], BLOCK))
+    hot, damp, order, own_sens = pl.pallas_call(
         functools.partial(select_body, ntx, nrx),
-        in_specs=[VMEM] * 4,
-        out_specs=[VMEM] * 3,
+        in_specs=[pl.BlockSpec(memory_space=pl.ANY)] * 4 + [VMEM] * 2,
+        out_specs=[VMEM] * 4,
         out_shape=[
             jax.ShapeDtypeStruct((rows, width), jnp.bfloat16),
             jax.ShapeDtypeStruct((1, rows), jnp.float32),
             jax.ShapeDtypeStruct((1, rows), jnp.int32),
+            jax.ShapeDtypeStruct((rows, half), jnp.bfloat16),
         ],
-        scratch_shapes=[pltpu.VMEM((width, rows), jnp.bfloat16)],
+        scratch_shapes=[
+            pltpu.VMEM((width, rows), jnp.bfloat16),
+            [pltpu.VMEM((rows,), jnp.int32)] * 3,
+            pltpu.VMEM((rows,), jnp.float32),
+            pltpu.SemaphoreType.DMA((4,)),
+        ],
         compiler_params=pltpu.CompilerParams(
-            vmem_limit_bytes=grant(((rows, width), 8), ((rows, STRIP), 8))
+            vmem_limit_bytes=grant(((rows, width), 8), ((rows, STRIP), 8), ((rows, half), 4))
         ),
         cost_estimate=pl.CostEstimate(
             flops=2 * width * rows * rows, bytes_accessed=4 * rows * width, transcendentals=0
         ),
-    )(panel_order, tx_of_row, rx_of_row, damping)
+    )(panel_order, tx_of_row, rx_of_row, damping, own, conds)
 
     strips = strips_of(rows)
     strip_shapes = [jax.ShapeDtypeStruct((rows - a, b - a), jnp.float32) for a, b in strips]
     lower = sum((rows - a) * (b - a) for a, b in strips)
-    conds = jnp.broadcast_to(layer_cond[:, None], (layer_cond.shape[0], BLOCK))
 
     def swap(value):
         return lax.ppermute(value, "grp", [(i, i ^ 1) for i in range(grp_count)])
@@ -430,7 +471,9 @@
         count = len(blocks)
         stacked = count > GROUP
         depth = half * (1 if stacked else min(count, GROUP))
-        args = [jnp.stack(blocks)] if stacked else blocks
+        begun = [] if sums else [own_sens]
+        args = [jnp.stack(blocks[len(begun) :])] if stacked else blocks[len(begun) :]
+        args = begun + args
         chosen = strips[:some]
         cost = 2 * count * half * (sum((rows - a) * (b - a) for a, b in chosen) + rows * STRIP * 2)
         sens = jax.ShapeDtypeStruct((rows, depth), jnp.bfloat16)
@@ -442,7 +485,6 @@
             out_shape=strip_shapes[:some] + [sens] * kept,
             scratch_shapes=([] if kept else [pltpu.VMEM(sens.shape, sens.dtype)])
             + [pltpu.VMEM((GROUP, 1, half), jnp.float32)],
-            input_output_aliases={2 + len(args) + i: i for i in range(len(sums[:some]))},
             compiler_params=pltpu.CompilerParams(
                 vmem_limit_bytes=grant(
                     ((lower,), 8), ((rows, depth), 2), ((rows, width), 2), ((count, own.size), 2)
@@ -472,7 +514,6 @@
                 in_specs=[VMEM] * (1 + len(others)),
                 out_specs=[VMEM] * len(others),
                 out_shape=strip_shapes[1:],
-                input_output_aliases={1 + i: i for i in range(len(others))},
                 compiler_params=pltpu.CompilerParams(
                     vmem_limit_bytes=grant(((lower,), 8), (sens.shape, 2))
                 ),

time: 83.6 us -> 78.3 us (0.937)
  the two profiles are of different devices: /device:TPU:0 before, /device:TPU:17 now
where the time goes in v1:
time: 78.3 us; the launch traced here: 77.9 us
  Pallas kernels  54.5 us (70%)
  starting transfers between devices  9.54 us (12%)
  local copies, waits for them, and re-layouts  6.68 us (9%)
  waiting for transfers between devices  6.3 us (8%)
    pallas_call x1, Pallas kernels, shards(): pl.pallas_call(functools.partial(finish_body, chosen_cols, cell_total, le...  26.3 us
    pallas_call x3, Pallas kernels, add(): pl.pallas_call(functools.partial(gram_body, ntx, nrx, count, stacked, not...  16.3 us
    ppermute x7, waiting for transfers between devices, along(): return lax.ppermute(value, 'tile', pairs)  6.29 us
    pallas_call x1, Pallas kernels, shards(): pl.pallas_call(functools.partial(start_body, cell_total), in_specs=[VMEM]...  6.23 us
    unnamed x18, local copies, waits for them, and re-layouts  5.95 us
    ppermute x7, starting transfers between devices, along(): return lax.ppermute(value, 'tile', pairs)  5.71 us
    ppermute x6, starting transfers between devices, swap(): return lax.ppermute(value, 'grp', [(i, i ^ 1) for i in range(grp_count)])  3.83 us
    pallas_call x1, Pallas kernels, shards(): pl.pallas_call(functools.partial(select_body, ntx, nrx), in_specs=[pl.Blo...  3.06 us
  transfers between devices with their start and end apart: 13, of which 2 were waited for; matrix products, arithmetic and copies ran while one was open for 1% of the time, Pallas kernels for 32%

profile of v1, /device:TPU:17, one launch (start us, length us, event | category | flops | bytes accessed | tf_op | source)
XLA Modules:
  0.0 77.9 jit_solution(1126961456235672500)
XLA Ops:
  0.6 0.0 copy-start
  0.6 0.9 %copy-done = bf16[128,1024]{1,0:T(8,128)(2,1)S(1)} copy-done((bf16[128,1024]{1,0:T(8,128)(2,1)S(1)}, bf16[128,1024]{1,0:T(8,128)(2,1)}, u32[]{:S(2)}) %copy-start) | copy-done | bytes 262168
  1.6 0.0 copy-start.1
  1.6 0.9 %copy-done.1 = bf16[64,1024]{1,0:T(8,128)(2,1)S(1)} copy-done((bf16[64,1024]{1,0:T(8,128)(2,1)S(1)}, bf16[64,1024]{1,0:T(8,128)(2,1)}, u32[]{:S(2)}) %copy-start.1) | copy-done | bytes 131096
  2.5 0.0 copy-start.2
  2.5 0.7 copy-done.2
  3.2 0.1 shard_map.95.own
  3.2 1.4 %collective-permute-start.3 = (bf16[208,512]{1,0:T(8,128)(2,1)S(1)}, bf16[208,512]{1,0:T(8,128)(2,1)S(1)}, u32[]{:S(2)}, u32[]{:S(2)}) collective-permute-start(bf16[208,512]{1,0:T(8,128)(2,1)S(1)} %shard_map.95.own), channel_id=1, source_target_pairs={{0,2},{1,3},{2,0},{3,1},{4,6},{5,7},{6,4},{7,5},{8,10},{9,11},{10,... | collective-permute-start | bytes 638984 | tf_op jit(solution)/shard_map/ppermute | solution.py:431
  4.6 1.2 %collective-permute-start.2 = (bf16[208,512]{1,0:T(8,128)(2,1)S(1)}, bf16[208,512]{1,0:T(8,128)(2,1)S(1)}, u32[]{:S(2)}, u32[]{:S(2)}) collective-permute-start(bf16[208,512]{1,0:T(8,128)(2,1)S(1)} %shard_map.95.own), channel_id=1, source_target_pairs={{0,1},{1,0},{2,3},{3,2},{4,5},{5,4},{6,7},{7,6},{8,9},{9,8},{10,11... | collective-permute-start | bytes 638984 | tf_op jit(solution)/shard_map/ppermute | solution.py:431
  5.8 0.1 collective-permute-start
  5.9 1.3 %collective-permute-start.1 = (bf16[208,512]{1,0:T(8,128)(2,1)S(1)}, bf16[208,512]{1,0:T(8,128)(2,1)S(1)}, u32[]{:S(2)}, u32[]{:S(2)}) collective-permute-start(bf16[208,512]{1,0:T(8,128)(2,1)S(1)} %shard_map.95.own), channel_id=1, source_target_pairs={{0,6},{1,7},{2,4},{3,5},{4,2},{5,3},{6,0},{7,1},{8,14},{9,15},{10,... | collective-permute-start | bytes 638984 | tf_op jit(solution)/shard_map/ppermute | solution.py:431
  7.2 0.7 broadcast_in_dim.2.layer_cond
  7.9 0.0 copy-start.5
  7.9 0.7 copy-done.5
  8.6 0.0 copy-start.6
  8.6 0.7 copy-done.6
  9.3 0.0 copy-start.7
  9.3 0.7 copy-done.7
  10.0 0.0 copy-start.8
  10.0 0.7 copy-done.8
  10.7 3.1 %shard_map.96 = (bf16[1408,256]{1,0:T(8,128)(2,1)S(1)}, f32[1,1408]{1,0:T(1,128)S(1)}, s32[1,1408]{1,0:T(1,128)S(1)}, bf16[1408,512]{1,0:T(8,128)(2,1)S(1)}) custom-call(s32[1408]{0:T(1024)S(1)} %copy-done.5, s32[1408]{0:T(1024)S(1)} %copy-done.6, s32[1408]{0:T(1024)S(1)} %copy-done.7, f32[1408]{0:T(1024)S(1)} %copy-done.8, ...), custom_call_target="tpu_custom_call" | custom-call | flops 1015021568 | bytes 1441792 | tf_op jit(solution)/shard_map/pallas_call | solution.py:439
  13.8 0.0 collective-permute-done.3.refs_2_
  13.8 0.3 collective-permute-start.6
  14.1 0.0 collective-permute-done.2.refs_1_
  14.1 6.0 %shard_map.97 = (f32[1408,256]{1,0:T(8,128)S(1)}, f32[1152,256]{1,0:T(8,128)S(1)}, f32[896,256]{1,0:T(8,128)S(1)}, f32[640,256]{1,0:T(8,128)S(1)}, f32[384,256]{1,0:T(8,128)S(1)}, /*index=5*/f32[128,128]{1,0:T(8,128)S(1)}) custom-call(bf16[1408,256]{1,0:T(8,128)(2,1)S(1)} %get-tuple-element.39.hot, f32[32,128]{1,0:T(8,128)S(1)} %broadcast_in_dim.2.layer_cond, ...), custom_call_target="tpu_custom_call" | custom-call | flops 5788139520 | bytes 9306112 | tf_op jit(solution)/shard_map/pallas_call | solution.py:481
  20.1 0.0 collective-permute-done.refs_0_
  20.2 5.2 %collective-permute-done.1.refs_1_ = bf16[208,512]{1,0:T(8,128)(2,1)S(1)} collective-permute-done((bf16[208,512]{1,0:T(8,128)(2,1)S(1)}, bf16[208,512]{1,0:T(8,128)(2,1)S(1)}, u32[]{:S(2)}, u32[]{:S(2)}) %collective-permute-start.1) | collective-permute-done | bytes 213024 | tf_op jit(solution)/shard_map/ppermute | solution.py:431
  25.3 0.0 collective-permute-start.4
  25.3 1.5 %collective-permute-start.5 = (bf16[208,512]{1,0:T(8,128)(2,1)S(1)}, bf16[208,512]{1,0:T(8,128)(2,1)S(1)}, u32[]{:S(2)}, u32[]{:S(2)}) collective-permute-start(bf16[208,512]{1,0:T(8,128)(2,1)S(1)} %collective-permute-done.1.refs_1_), channel_id=1, source_target_pairs={{0,1},{1,0},{2,3},{3,2},{4,5},{5,4},{6,7},{7,6},{8,9},{9,8},{10,11... | collective-permute-start | bytes 638984 | tf_op jit(solution)/shard_map/ppermute | solution.py:431
  26.8 0.0 collective-permute-done.6.refs_2_
  26.8 6.9 %shard_map.98 = (f32[1408,256]{1,0:T(8,128)S(1)}, f32[1152,256]{1,0:T(8,128)S(1)}, f32[896,256]{1,0:T(8,128)S(1)}, f32[640,256]{1,0:T(8,128)S(1)}, f32[384,256]{1,0:T(8,128)S(1)}, /*index=5*/f32[128,128]{1,0:T(8,128)S(1)}) custom-call(bf16[1408,256]{1,0:T(8,128)(2,1)S(1)} %get-tuple-element.39.hot, f32[32,128]{1,0:T(8,128)S(1)} %broadcast_in_dim.2.layer_cond, ...), custom_call_target="tpu_custom_call" | custom-call | flops 5788139520 | bytes 9306112 | tf_op jit(solution)/shard_map/pallas_call | solution.py:481
  33.7 0.0 collective-permute-done.4.refs_0_
  33.7 1.1 %collective-permute-done.5.refs_1_ = bf16[208,512]{1,0:T(8,128)(2,1)S(1)} collective-permute-done((bf16[208,512]{1,0:T(8,128)(2,1)S(1)}, bf16[208,512]{1,0:T(8,128)(2,1)S(1)}, u32[]{:S(2)}, u32[]{:S(2)}) %collective-permute-start.5) | collective-permute-done | bytes 213024 | tf_op jit(solution)/shard_map/ppermute | solution.py:431
  34.8 3.3 %shard_map.99 = (f32[1408,256]{1,0:T(8,128)S(1)}, bf16[1408,1024]{1,0:T(8,128)(2,1)S(1)}) custom-call(bf16[1408,256]{1,0:T(8,128)(2,1)S(1)} %get-tuple-element.39.hot, f32[32,128]{1,0:T(8,128)S(1)} %broadcast_in_dim.2.layer_cond, bf16[208,512]{1,0:T(8,128)(2,1)S(1)} %collective-permute-done.4.refs_0_, bf16[208,512]{1,0:T(8,128)(2,1)S(1)} %collective-permute-done.5.refs_1_, ...), custom_call_target="tpu_custom_call" | custom-call | flops 2214592512 | bytes 9306112 | tf_op jit(solution)/shard_map/pallas_call | solution.py:481
  38.2 2.8 %collective-permute-start.7 = (f32[1408,256]{1,0:T(8,128)S(1)}, f32[1408,256]{1,0:T(8,128)S(1)}, u32[]{:S(2)}, u32[]{:S(2)}) collective-permute-start(f32[1408,256]{1,0:T(8,128)S(1)} %get-tuple-element.56.mine), channel_id=1, source_target_pairs={{0,8},{8,0},{16,24},{24,16},{1,9},{9,1},{17,25},{25,17},{2,10},{10... | collective-permute-start | bytes 4325384 | tf_op jit(solution)/shard_map/ppermute | solution.py:468
  41.0 2.6 %shard_map.101 = (f32[1152,256]{1,0:T(8,128)}, f32[896,256]{1,0:T(8,128)}, f32[640,256]{1,0:T(8,128)S(1)}, f32[384,256]{1,0:T(8,128)}, f32[128,128]{1,0:T(8,128)S(1)}) custom-call(bf16[1408,1024]{1,0:T(8,128)(2,1)S(1)} %get-tuple-element.59.sens, f32[1152,256]{1,0:T(8,128)S(1)} %get-tuple-element.60.refs_0_, f32[896,256]{1,0:T(8,128)S(1)} %get-tuple-element.61.refs_1_, ...), custom_call_target="tpu_custom_call" | custom-call | flops 2382364672 | bytes 9306112 | tf_op jit(solution)/shard_map/pallas_call | solution.py:512
  43.6 0.0 copy-start.3
  43.6 0.6 copy-done.3
  44.2 0.0 collective-permute-start.8
  44.2 0.5 collective-permute-start.9
  44.7 0.0 collective-permute-start.10
  44.8 0.5 collective-permute-start.11
  45.2 0.1 pad_add_fusion.place
  45.3 0.0 collective-permute-done.7.theirs
  45.3 0.0 collective-permute-start.12
  45.3 0.0 copy-start.4
  45.3 6.2 %shard_map.100 = (bf16[1408,256]{1,0:T(8,128)(2,1)S(1)}, bf16[1408,256]{1,0:T(8,128)(2,1)S(1)}) custom-call(f32[1,1408]{1,0:T(1,128)S(1)} %get-tuple-element.37.damping, f32[1408,256]{1,0:T(8,128)S(1)} %get-tuple-element.56.mine, f32[1408,256]{1,0:T(8,128)S(1)} %collective-permute-done.7.theirs), custom_call_target="tpu_custom_call" | custom-call | flops 2952790016 | bytes 2883584 | tf_op jit(solution)/shard_map/pallas_call | solution.py:535
  51.6 0.0 collective-permute-done.12.refs_9_
  51.6 0.0 collective-permute-done.11.refs_8_
  51.6 0.0 collective-permute-done.10.refs_7_
  51.6 0.0 collective-permute-done.9.refs_6_
  51.6 0.0 collective-permute-done.8.refs_5_
  51.6 0.0 copy-done.4
  51.7 26.3 %shard_map.102 = (f32[176,352]{1,0:T(8,128)}, f32[352,1024]{1,0:T(8,128)}) custom-call(s32[2]{0:T(128)S(1)} %pad_add_fusion.place, f32[1,1408]{1,0:T(1,128)S(1)} %get-tuple-element.37.damping, s32[1,1408]{1,0:T(1,128)S(1)} %get-tuple-element.38.order, bf16[1408,256]{1,0:T(8,128)(2,1)S(1)} %get-tuple-element.57.high, ...), custom_call_target="tpu_custom_call" | custom-call | flops 12180258816 | bytes 9306112 | tf_op jit(solution)/shard_map/pallas_call | solution.py:552
Async XLA Ops:
  0.6 1.0 %copy-start = (bf16[128,1024]{1,0:T(8,128)(2,1)S(1)}, bf16[128,1024]{1,0:T(8,128)(2,1)}, u32[]{:S(2)}) copy-start(bf16[128,1024]{1,0:T(8,128)(2,1)} %rx_fields.1) | copy-start | bytes 786436
  1.6 0.9 %copy-start.1 = (bf16[64,1024]{1,0:T(8,128)(2,1)S(1)}, bf16[64,1024]{1,0:T(8,128)(2,1)}, u32[]{:S(2)}) copy-start(bf16[64,1024]{1,0:T(8,128)(2,1)} %tx_fields.1) | copy-start | bytes 393220
  2.5 0.7 copy-start.2
  3.2 10.5 %collective-permute-start.3 = (bf16[208,512]{1,0:T(8,128)(2,1)S(1)}, bf16[208,512]{1,0:T(8,128)(2,1)S(1)}, u32[]{:S(2)}, u32[]{:S(2)}) collective-permute-start(bf16[208,512]{1,0:T(8,128)(2,1)S(1)} %shard_map.95.own), channel_id=1, source_target_pairs={{0,2},{1,3},{2,0},{3,1},{4,6},{5,7},{6,4},{7,5},{8,10},{9,11},{10,... | collective-permute-start | bytes 638984 | tf_op jit(solution)/shard_map/ppermute | solution.py:431
  4.6 9.5 %collective-permute-start.2 = (bf16[208,512]{1,0:T(8,128)(2,1)S(1)}, bf16[208,512]{1,0:T(8,128)(2,1)S(1)}, u32[]{:S(2)}, u32[]{:S(2)}) collective-permute-start(bf16[208,512]{1,0:T(8,128)(2,1)S(1)} %shard_map.95.own), channel_id=1, source_target_pairs={{0,1},{1,0},{2,3},{3,2},{4,5},{5,4},{6,7},{7,6},{8,9},{9,8},{10,11... | collective-permute-start | bytes 638984 | tf_op jit(solution)/shard_map/ppermute | solution.py:431
  5.8 14.3 %collective-permute-start = (bf16[208,512]{1,0:T(8,128)(2,1)S(1)}, bf16[208,512]{1,0:T(8,128)(2,1)S(1)}, u32[]{:S(2)}, u32[]{:S(2)}) collective-permute-start(bf16[208,512]{1,0:T(8,128)(2,1)S(1)} %shard_map.95.own), channel_id=1, source_target_pairs={{0,4},{1,5},{2,6},{3,7},{4,0},{5,1},{6,2},{7,3},{8,12},{9,13},{10,... | collective-permute-start | bytes 638984 | tf_op jit(solution)/shard_map/ppermute | solution.py:431
  5.9 19.4 %collective-permute-start.1 = (bf16[208,512]{1,0:T(8,128)(2,1)S(1)}, bf16[208,512]{1,0:T(8,128)(2,1)S(1)}, u32[]{:S(2)}, u32[]{:S(2)}) collective-permute-start(bf16[208,512]{1,0:T(8,128)(2,1)S(1)} %shard_map.95.own), channel_id=1, source_target_pairs={{0,6},{1,7},{2,4},{3,5},{4,2},{5,3},{6,0},{7,1},{8,14},{9,15},{10,... | collective-permute-start | bytes 638984 | tf_op jit(solution)/shard_map/ppermute | solution.py:431
  7.9 0.7 copy-start.5
  8.6 0.7 copy-start.6
  9.3 0.7 copy-start.7
  10.0 0.7 copy-start.8
  13.8 13.0 %collective-permute-start.6 = (bf16[208,512]{1,0:T(8,128)(2,1)S(1)}, bf16[208,512]{1,0:T(8,128)(2,1)S(1)}, u32[]{:S(2)}, u32[]{:S(2)}) collective-permute-start(bf16[208,512]{1,0:T(8,128)(2,1)S(1)} %collective-permute-done.3.refs_2_), channel_id=1, source_target_pairs={{0,1},{1,0},{2,3},{3,2},{4,5},{5,4},{6,7},{7,6},{8,9},{9,8},{10,11... | collective-permute-start | bytes 638984 | tf_op jit(solution)/shard_map/ppermute | solution.py:431
  25.3 8.4 %collective-permute-start.4 = (bf16[208,512]{1,0:T(8,128)(2,1)S(1)}, bf16[208,512]{1,0:T(8,128)(2,1)S(1)}, u32[]{:S(2)}, u32[]{:S(2)}) collective-permute-start(bf16[208,512]{1,0:T(8,128)(2,1)S(1)} %collective-permute-done.refs_0_), channel_id=1, source_target_pairs={{0,1},{1,0},{2,3},{3,2},{4,5},{5,4},{6,7},{7,6},{8,9},{9,8},{10,11... | collective-permute-start | bytes 638984 | tf_op jit(solution)/shard_map/ppermute | solution.py:431
  25.3 9.5 %collective-permute-start.5 = (bf16[208,512]{1,0:T(8,128)(2,1)S(1)}, bf16[208,512]{1,0:T(8,128)(2,1)S(1)}, u32[]{:S(2)}, u32[]{:S(2)}) collective-permute-start(bf16[208,512]{1,0:T(8,128)(2,1)S(1)} %collective-permute-done.1.refs_1_), channel_id=1, source_target_pairs={{0,1},{1,0},{2,3},{3,2},{4,5},{5,4},{6,7},{7,6},{8,9},{9,8},{10,11... | collective-permute-start | bytes 638984 | tf_op jit(solution)/shard_map/ppermute | solution.py:431
  38.2 7.2 %collective-permute-start.7 = (f32[1408,256]{1,0:T(8,128)S(1)}, f32[1408,256]{1,0:T(8,128)S(1)}, u32[]{:S(2)}, u32[]{:S(2)}) collective-permute-start(f32[1408,256]{1,0:T(8,128)S(1)} %get-tuple-element.56.mine), channel_id=1, source_target_pairs={{0,8},{8,0},{16,24},{24,16},{1,9},{9,1},{17,25},{25,17},{2,10},{10... | collective-permute-start | bytes 4325384 | tf_op jit(solution)/shard_map/ppermute | solution.py:468
  43.6 0.6 copy-start.3
  44.2 7.4 %collective-permute-start.8 = (f32[1152,256]{1,0:T(8,128)}, f32[1152,256]{1,0:T(8,128)}, u32[]{:S(2)}, u32[]{:S(2)}) collective-permute-start(f32[1152,256]{1,0:T(8,128)} %get-tuple-element.65.refs_0_), channel_id=1, source_target_pairs={{0,8},{8,0},{16,24},{24,16},{1,9},{9,1},{17,25},{25,17},{2,10},{10... | collective-permute-start | bytes 3538952 | tf_op jit(solution)/shard_map/ppermute | solution.py:468
  44.2 7.4 %collective-permute-start.9 = (f32[896,256]{1,0:T(8,128)}, f32[896,256]{1,0:T(8,128)}, u32[]{:S(2)}, u32[]{:S(2)}) collective-permute-start(f32[896,256]{1,0:T(8,128)} %get-tuple-element.66.refs_1_), channel_id=1, source_target_pairs={{0,8},{8,0},{16,24},{24,16},{1,9},{9,1},{17,25},{25,17},{2,10},{10... | collective-permute-start | bytes 2752520 | tf_op jit(solution)/shard_map/ppermute | solution.py:468
  44.7 6.9 %collective-permute-start.10 = (f32[640,256]{1,0:T(8,128)S(1)}, f32[640,256]{1,0:T(8,128)}, u32[]{:S(2)}, u32[]{:S(2)}) collective-permute-start(f32[640,256]{1,0:T(8,128)S(1)} %get-tuple-element.67.refs_2_), channel_id=1, source_target_pairs={{0,8},{8,0},{16,24},{24,16},{1,9},{9,1},{17,25},{25,17},{2,10},{10... | collective-permute-start | bytes 1966088 | tf_op jit(solution)/shard_map/ppermute | solution.py:468
  44.8 6.9 %collective-permute-start.11 = (f32[384,256]{1,0:T(8,128)}, f32[384,256]{1,0:T(8,128)}, u32[]{:S(2)}, u32[]{:S(2)}) collective-permute-start(f32[384,256]{1,0:T(8,128)} %get-tuple-element.68.refs_3_), channel_id=1, source_target_pairs={{0,8},{8,0},{16,24},{24,16},{1,9},{9,1},{17,25},{25,17},{2,10},{10... | collective-permute-start | bytes 1179656 | tf_op jit(solution)/shard_map/ppermute | solution.py:468
  45.3 6.3 %collective-permute-start.12 = (f32[128,128]{1,0:T(8,128)}, f32[128,128]{1,0:T(8,128)S(1)}, u32[]{:S(2)}, u32[]{:S(2)}) collective-permute-start(f32[128,128]{1,0:T(8,128)} %copy-done.3), channel_id=1, source_target_pairs={{0,8},{8,0},{16,24},{24,16},{1,9},{9,1},{17,25},{25,17},{2,10},{10... | collective-permute-start | bytes 196616 | tf_op jit(solution)/shard_map/ppermute | solution.py:468
  45.3 6.3 %copy-start.4 = (f32[128,128]{1,0:T(8,128)S(1)}, f32[128,128]{1,0:T(8,128)}, u32[]{:S(2)}) copy-start(f32[128,128]{1,0:T(8,128)} %copy-done.3) | copy-start | bytes 196612

commit v2 on v1

--- a/solution.py
+++ b/solution.py
@@ -13,6 +13,7 @@
 STEP = 16
 STRIP = 256
 PARTS = 4
+EMITS = 2
 GROUP = 3
 PAD = 16
 VMEM = pl.BlockSpec(memory_space=pltpu.VMEM)
@@ -122,30 +123,19 @@
 
 
 def select_body(
-    ntx, nrx, order, tx_of_row, rx_of_row, damping, own, layer_cond, hot, damp, line, sens, table, ints, floats, sems
+    ntx, nrx, vectors, damping, own, layer_cond, hot, damp, line, sens, table
 ):
-    rows = order.shape[0]
-    copies = [
-        pltpu.make_async_copy(source, target, sems.at[i])
-        for i, (source, target) in enumerate(
-            zip((order, tx_of_row, rx_of_row, damping), list(ints) + [floats])
-        )
-    ]
-    for copy in copies:
-        copy.start()
-    for copy in copies:
-        copy.wait()
-    order, tx_of_row, rx_of_row = ints
-    damping = floats
+    rows = vectors.shape[1]
+    order, tx_of_row, rx_of_row = (vectors[i : i + 1, :] for i in range(3))
+    damping = damping[...].reshape(1, rows)
     table[:ntx, :] = (
-        lax.broadcasted_iota(jnp.int32, (ntx, rows), 0) == tx_of_row[...].reshape(1, rows)
+        lax.broadcasted_iota(jnp.int32, (ntx, rows), 0) == tx_of_row
     ).astype(jnp.bfloat16)
     table[ntx : ntx + nrx, :] = (
-        lax.broadcasted_iota(jnp.int32, (nrx, rows), 0) == rx_of_row[...].reshape(1, rows)
+        lax.broadcasted_iota(jnp.int32, (nrx, rows), 0) == rx_of_row
     ).astype(jnp.bfloat16)
-    line[...] = order[...].reshape(1, rows)
+    line[...] = order
     spare = table.shape[0] - ntx - nrx
-    damping = damping[...].reshape(1, rows)
     high = damping.astype(jnp.bfloat16).astype(jnp.float32)
     middle, low = halves(damping - high)
     which = lax.broadcasted_iota(jnp.int32, (spare, rows), 0)
@@ -333,7 +323,7 @@
     mine, refs = refs[:count], refs[count:]
     theirs, refs = refs[:count], refs[count:]
     trailing, factor, refs = refs[0], refs[1], refs[2:]
-    state, row_hot, pairs = refs[:5], refs[5], refs[6:]
+    state, row_hot, rows_pairs, pairs = refs[:5], refs[5], refs[6], refs[7:]
     rows = order.shape[1]
     scale = 1.0 / cell_total
     pairs = [(high, low)] + list(zip(pairs[::2], pairs[1::2]))
@@ -350,19 +340,27 @@
             place[1] + lax.broadcasted_iota(jnp.int32, (tile_cols, b - a), 0) == order[:, a:b]
         ).astype(jnp.bfloat16)
 
-    def emit(s):
+    def emit(s, part):
         at, end = s * STRIP, (s + 1) * STRIP
         high, low = pairs[s]
-        rows_high = dot(row_hot[:, at:], high[...], PLAIN)
-        rows_low = dot(row_hot[:, at:], low[...], PLAIN)
-        factor[:, at:end] = rows_high + rows_low
-        kept = jnp.sum(row_hot[:, chosen_cols:].astype(jnp.float32), axis=1, keepdims=True)
+        size = group_rows // EMITS
+        here = slice(part * size, (part + 1) * size)
+        rows_high = dot(row_hot[here, at:], high[...], PLAIN)
+        rows_low = dot(row_hot[here, at:], low[...], PLAIN)
+        factor[here, at:end] = rows_high + rows_low
+        kept = jnp.sum(row_hot[here, chosen_cols:].astype(jnp.float32), axis=1, keepdims=True)
+        rows_pairs[0, here, :] = (rows_high * kept).astype(jnp.bfloat16)
+        rows_pairs[1, here, :] = (rows_low * kept).astype(jnp.bfloat16)
+
+    def subtract(s):
+        high, low = pairs[s]
+        at = s * STRIP
         picks = col_hot(chosen_cols, rows)
         cols_high = dot(picks, high[chosen_cols - at :, :], PLAIN)
         cols_low = dot(picks, low[chosen_cols - at :, :], PLAIN)
         trailing[...] -= product(
             (cols_high.astype(jnp.bfloat16), cols_low.astype(jnp.bfloat16)),
-            ((rows_high * kept).astype(jnp.bfloat16), (rows_low * kept).astype(jnp.bfloat16)),
+            (rows_pairs[0], rows_pairs[1]),
             ROWS_ROWS,
         )
 
@@ -384,13 +382,17 @@
     calls = {k: [] for k in range(per, last)}
     calls[per].append(place_rows)
     for s in range(len(pairs) - 1):
-        calls[min((s + 1) * per + 1, last - 1)].append(functools.partial(emit, s))
+        for part in range(EMITS):
+            calls[min((s + 1) * per + 1, last - 1)].append(functools.partial(emit, s, part))
+        calls[min((s + 1) * per + 1, last - 1)].append(functools.partial(subtract, s))
     for i, (at, end) in enumerate((a, b) for a, b in strips_of(rows) if a >= chosen_cols):
         calls[max(per + 1, last - 1 - i % 2 * per)].append(functools.partial(remain, at, end))
     factor_columns(
         per, last, rows, scale, mine, theirs, damping, Panels(pairs), state, lambda k: calls[k]
     )
-    emit(len(pairs) - 1)
+    for part in range(EMITS):
+        emit(len(pairs) - 1, part)
+    subtract(len(pairs) - 1)
 
 
 def shards(
@@ -430,6 +432,7 @@
             pairs.append((i, o * inner + n))
         return lax.ppermute(value, "tile", pairs)
 
+    vectors = jnp.stack([panel_order, tx_of_row, rx_of_row])
     near = [along(own, (0, k)) for k in range(1, inner)]
     far = [along(own, (k, 0)) for k in range(1, outer)]
     relayed = [[along(far[0], (0, k)) for k in range(1, inner)]]
@@ -438,7 +441,7 @@
     conds = jnp.broadcast_to(layer_cond[:, None], (layer_cond.shape[0], BLOCK))
     hot, damp, order, own_sens = pl.pallas_call(
         functools.partial(select_body, ntx, nrx),
-        in_specs=[pl.BlockSpec(memory_space=pl.ANY)] * 4 + [VMEM] * 2,
+        in_specs=[VMEM] * 4,
         out_specs=[VMEM] * 4,
         out_shape=[
             jax.ShapeDtypeStruct((rows, width), jnp.bfloat16),
@@ -446,19 +449,14 @@
             jax.ShapeDtypeStruct((1, rows), jnp.int32),
             jax.ShapeDtypeStruct((rows, half), jnp.bfloat16),
         ],
-        scratch_shapes=[
-            pltpu.VMEM((width, rows), jnp.bfloat16),
-            [pltpu.VMEM((rows,), jnp.int32)] * 3,
-            pltpu.VMEM((rows,), jnp.float32),
-            pltpu.SemaphoreType.DMA((4,)),
-        ],
+        scratch_shapes=[pltpu.VMEM((width, rows), jnp.bfloat16)],
         compiler_params=pltpu.CompilerParams(
             vmem_limit_bytes=grant(((rows, width), 8), ((rows, STRIP), 8), ((rows, half), 4))
         ),
         cost_estimate=pl.CostEstimate(
             flops=2 * width * rows * rows, bytes_accessed=4 * rows * width, transcendentals=0
         ),
-    )(panel_order, tx_of_row, rx_of_row, damping, own, conds)
+    )(vectors, damping, own, conds)
 
     strips = strips_of(rows)
     strip_shapes = [jax.ShapeDtypeStruct((rows - a, b - a), jnp.float32) for a, b in strips]
@@ -559,6 +557,7 @@
             ],
             scratch_shapes=state
             + [pltpu.VMEM((group_rows, rows), jnp.bfloat16)]
+            + [pltpu.VMEM((2, group_rows, STRIP), jnp.bfloat16)]
             + [pltpu.VMEM(shape, jnp.bfloat16) for shape in later for _ in range(2)],
             compiler_params=pltpu.CompilerParams(
                 vmem_limit_bytes=grant(

time: 78.3 us -> 77.3 us (0.987)
  Pallas kernels: 54.5 us -> 53.5 us
    another operation x0 -> x3, local copies, waits for them, and re-layouts: none -> 2.1 us  [shards(): vectors = jnp.stack([panel_order, tx_of_row, rx_of_row])]
    unnamed x18 -> x12, local copies, waits for them, and re-layouts: 5.95 us -> 3.86 us
    pallas_call x1, Pallas kernels: 26.3 us -> 25.3 us  [shards(): pl.pallas_call(functools.partial(finish_body, chosen_cols, cell_total, le...]
  transfers between devices with their start and end apart: 13 -> 13, of which waited for: 2 -> 2; matrix products, arithmetic and copies ran while one was open for 1% -> 4% of each run, Pallas kernels for 32% -> 32%
where the time goes in v2:
time: 77.3 us; the launch traced here: 76.9 us
  Pallas kernels  53.5 us (69%)
  starting transfers between devices  9.54 us (12%)
  local copies, waits for them, and re-layouts  6.69 us (9%)
  waiting for transfers between devices  6.34 us (8%)
  between operations  0.78 us (1%)
    pallas_call x1, Pallas kernels, shards(): pl.pallas_call(functools.partial(finish_body, chosen_cols, cell_total, le...  25.3 us
    pallas_call x3, Pallas kernels, add(): pl.pallas_call(functools.partial(gram_body, ntx, nrx, count, stacked, not...  16.3 us
    ppermute x7, waiting for transfers between devices, along(): return lax.ppermute(value, 'tile', pairs)  6.32 us
    pallas_call x1, Pallas kernels, shards(): pl.pallas_call(functools.partial(start_body, cell_total), in_specs=[VMEM]...  6.23 us
    ppermute x7, starting transfers between devices, along(): return lax.ppermute(value, 'tile', pairs)  5.71 us
    unnamed x12, local copies, waits for them, and re-layouts  3.86 us
    ppermute x6, starting transfers between devices, swap(): return lax.ppermute(value, 'grp', [(i, i ^ 1) for i in range(grp_count)])  3.83 us
    pallas_call x1, Pallas kernels, shards(): pl.pallas_call(functools.partial(select_body, ntx, nrx), in_specs=[VMEM]...  2.99 us
  transfers between devices with their start and end apart: 13, of which 2 were waited for; matrix products, arithmetic and copies ran while one was open for 4% of the time, Pallas kernels for 32%

profile of v2, /device:TPU:17, one launch (start us, length us, event | category | flops | bytes accessed | tf_op | source)
XLA Modules:
  0.0 76.9 jit_solution(15191440570945795339)
XLA Ops:
  0.6 0.0 copy-start
  0.6 0.9 %copy-done = bf16[128,1024]{1,0:T(8,128)(2,1)S(1)} copy-done((bf16[128,1024]{1,0:T(8,128)(2,1)S(1)}, bf16[128,1024]{1,0:T(8,128)(2,1)}, u32[]{:S(2)}) %copy-start) | copy-done | bytes 262168
  1.6 0.0 copy-start.1
  1.6 0.9 %copy-done.1 = bf16[64,1024]{1,0:T(8,128)(2,1)S(1)} copy-done((bf16[64,1024]{1,0:T(8,128)(2,1)S(1)}, bf16[64,1024]{1,0:T(8,128)(2,1)}, u32[]{:S(2)}) %copy-start.1) | copy-done | bytes 131096
  2.5 0.0 copy-start.2
  2.5 0.7 copy-done.2
  3.2 0.1 shard_map.95.own
  3.2 1.4 %collective-permute-start.3 = (bf16[208,512]{1,0:T(8,128)(2,1)S(1)}, bf16[208,512]{1,0:T(8,128)(2,1)S(1)}, u32[]{:S(2)}, u32[]{:S(2)}) collective-permute-start(bf16[208,512]{1,0:T(8,128)(2,1)S(1)} %shard_map.95.own), channel_id=1, source_target_pairs={{0,2},{1,3},{2,0},{3,1},{4,6},{5,7},{6,4},{7,5},{8,10},{9,11},{10,... | collective-permute-start | bytes 638984 | tf_op jit(solution)/shard_map/ppermute | solution.py:433
  4.6 1.2 %collective-permute-start.2 = (bf16[208,512]{1,0:T(8,128)(2,1)S(1)}, bf16[208,512]{1,0:T(8,128)(2,1)S(1)}, u32[]{:S(2)}, u32[]{:S(2)}) collective-permute-start(bf16[208,512]{1,0:T(8,128)(2,1)S(1)} %shard_map.95.own), channel_id=1, source_target_pairs={{0,1},{1,0},{2,3},{3,2},{4,5},{5,4},{6,7},{7,6},{8,9},{9,8},{10,11... | collective-permute-start | bytes 638984 | tf_op jit(solution)/shard_map/ppermute | solution.py:433
  5.8 0.1 collective-permute-start
  5.9 1.3 %collective-permute-start.1 = (bf16[208,512]{1,0:T(8,128)(2,1)S(1)}, bf16[208,512]{1,0:T(8,128)(2,1)S(1)}, u32[]{:S(2)}, u32[]{:S(2)}) collective-permute-start(bf16[208,512]{1,0:T(8,128)(2,1)S(1)} %shard_map.95.own), channel_id=1, source_target_pairs={{0,6},{1,7},{2,4},{3,5},{4,2},{5,3},{6,0},{7,1},{8,14},{9,15},{10,... | collective-permute-start | bytes 638984 | tf_op jit(solution)/shard_map/ppermute | solution.py:433
  7.2 0.7 stack.24
  7.9 0.7 stack.25
  8.6 0.7 stack.26
  9.3 0.7 broadcast_in_dim.2.layer_cond
  10.1 0.0 copy-start.5
  10.1 0.7 copy-done.5
  10.8 3.0 %shard_map.96 = (bf16[1408,256]{1,0:T(8,128)(2,1)S(1)}, f32[1,1408]{1,0:T(1,128)S(1)}, s32[1,1408]{1,0:T(1,128)S(1)}, bf16[1408,512]{1,0:T(8,128)(2,1)S(1)}) custom-call(s32[3,1408]{1,0:T(4,128)S(1)} %pad_add_fusion.vectors, f32[1408]{0:T(1024)S(1)} %copy-done.5, bf16[208,512]{1,0:T(8,128)(2,1)S(1)} %shard_map.95.own, f32[32,128]{1,0:T(8,128)S(1)} %broadcast_in_dim.2.layer_cond), custom_call_target="tpu_custom_call" | custom-call | flops 1015021568 | bytes 1441792 | tf_op jit(solution)/shard_map/pallas_call | solution.py:442
  13.8 0.0 collective-permute-done.3.refs_2_
  13.8 0.3 collective-permute-start.6
  14.1 0.0 collective-permute-done.2.refs_1_
  14.1 6.0 %shard_map.97 = (f32[1408,256]{1,0:T(8,128)S(1)}, f32[1152,256]{1,0:T(8,128)S(1)}, f32[896,256]{1,0:T(8,128)S(1)}, f32[640,256]{1,0:T(8,128)S(1)}, f32[384,256]{1,0:T(8,128)S(1)}, /*index=5*/f32[128,128]{1,0:T(8,128)S(1)}) custom-call(bf16[1408,256]{1,0:T(8,128)(2,1)S(1)} %get-tuple-element.39.hot, f32[32,128]{1,0:T(8,128)S(1)} %broadcast_in_dim.2.layer_cond, ...), custom_call_target="tpu_custom_call" | custom-call | flops 5788139520 | bytes 9306112 | tf_op jit(solution)/shard_map/pallas_call | solution.py:479
  20.1 0.0 collective-permute-done.refs_0_
  20.1 5.2 %collective-permute-done.1.refs_1_ = bf16[208,512]{1,0:T(8,128)(2,1)S(1)} collective-permute-done((bf16[208,512]{1,0:T(8,128)(2,1)S(1)}, bf16[208,512]{1,0:T(8,128)(2,1)S(1)}, u32[]{:S(2)}, u32[]{:S(2)}) %collective-permute-start.1) | collective-permute-done | bytes 213024 | tf_op jit(solution)/shard_map/ppermute | solution.py:433
  25.3 0.0 collective-permute-start.4
  25.3 1.5 %collective-permute-start.5 = (bf16[208,512]{1,0:T(8,128)(2,1)S(1)}, bf16[208,512]{1,0:T(8,128)(2,1)S(1)}, u32[]{:S(2)}, u32[]{:S(2)}) collective-permute-start(bf16[208,512]{1,0:T(8,128)(2,1)S(1)} %collective-permute-done.1.refs_1_), channel_id=1, source_target_pairs={{0,1},{1,0},{2,3},{3,2},{4,5},{5,4},{6,7},{7,6},{8,9},{9,8},{10,11... | collective-permute-start | bytes 638984 | tf_op jit(solution)/shard_map/ppermute | solution.py:433
  26.8 0.0 collective-permute-done.6.refs_2_
  26.8 6.9 %shard_map.98 = (f32[1408,256]{1,0:T(8,128)S(1)}, f32[1152,256]{1,0:T(8,128)S(1)}, f32[896,256]{1,0:T(8,128)S(1)}, f32[640,256]{1,0:T(8,128)S(1)}, f32[384,256]{1,0:T(8,128)S(1)}, /*index=5*/f32[128,128]{1,0:T(8,128)S(1)}) custom-call(bf16[1408,256]{1,0:T(8,128)(2,1)S(1)} %get-tuple-element.39.hot, f32[32,128]{1,0:T(8,128)S(1)} %broadcast_in_dim.2.layer_cond, ...), custom_call_target="tpu_custom_call" | custom-call | flops 5788139520 | bytes 9306112 | tf_op jit(solution)/shard_map/pallas_call | solution.py:479
  33.7 0.0 collective-permute-done.4.refs_0_
  33.7 1.1 %collective-permute-done.5.refs_1_ = bf16[208,512]{1,0:T(8,128)(2,1)S(1)} collective-permute-done((bf16[208,512]{1,0:T(8,128)(2,1)S(1)}, bf16[208,512]{1,0:T(8,128)(2,1)S(1)}, u32[]{:S(2)}, u32[]{:S(2)}) %collective-permute-start.5) | collective-permute-done | bytes 213024 | tf_op jit(solution)/shard_map/ppermute | solution.py:433
  34.8 3.3 %shard_map.99 = (f32[1408,256]{1,0:T(8,128)S(1)}, bf16[1408,1024]{1,0:T(8,128)(2,1)S(1)}) custom-call(bf16[1408,256]{1,0:T(8,128)(2,1)S(1)} %get-tuple-element.39.hot, f32[32,128]{1,0:T(8,128)S(1)} %broadcast_in_dim.2.layer_cond, bf16[208,512]{1,0:T(8,128)(2,1)S(1)} %collective-permute-done.4.refs_0_, bf16[208,512]{1,0:T(8,128)(2,1)S(1)} %collective-permute-done.5.refs_1_, ...), custom_call_target="tpu_custom_call" | custom-call | flops 2214592512 | bytes 9306112 | tf_op jit(solution)/shard_map/pallas_call | solution.py:479
  38.2 2.8 %collective-permute-start.7 = (f32[1408,256]{1,0:T(8,128)S(1)}, f32[1408,256]{1,0:T(8,128)S(1)}, u32[]{:S(2)}, u32[]{:S(2)}) collective-permute-start(f32[1408,256]{1,0:T(8,128)S(1)} %get-tuple-element.56.mine), channel_id=1, source_target_pairs={{0,8},{8,0},{16,24},{24,16},{1,9},{9,1},{17,25},{25,17},{2,10},{10... | collective-permute-start | bytes 4325384 | tf_op jit(solution)/shard_map/ppermute | solution.py:466
  41.0 2.6 %shard_map.101 = (f32[1152,256]{1,0:T(8,128)}, f32[896,256]{1,0:T(8,128)}, f32[640,256]{1,0:T(8,128)S(1)}, f32[384,256]{1,0:T(8,128)}, f32[128,128]{1,0:T(8,128)S(1)}) custom-call(bf16[1408,1024]{1,0:T(8,128)(2,1)S(1)} %get-tuple-element.59.sens, f32[1152,256]{1,0:T(8,128)S(1)} %get-tuple-element.60.refs_0_, f32[896,256]{1,0:T(8,128)S(1)} %get-tuple-element.61.refs_1_, ...), custom_call_target="tpu_custom_call" | custom-call | flops 2382364672 | bytes 9306112 | tf_op jit(solution)/shard_map/pallas_call | solution.py:510
  43.6 0.0 copy-start.3
  43.6 0.6 copy-done.3
  44.2 0.0 collective-permute-start.8
  44.2 0.5 collective-permute-start.9
  44.7 0.0 collective-permute-start.10
  44.8 0.5 collective-permute-start.11
  45.2 0.1 pad_add_fusion.1.place
  45.3 0.0 collective-permute-done.7.theirs
  45.3 0.0 collective-permute-start.12
  45.3 0.0 copy-start.4
  45.3 6.2 %shard_map.100 = (bf16[1408,256]{1,0:T(8,128)(2,1)S(1)}, bf16[1408,256]{1,0:T(8,128)(2,1)S(1)}) custom-call(f32[1,1408]{1,0:T(1,128)S(1)} %get-tuple-element.37.damping, f32[1408,256]{1,0:T(8,128)S(1)} %get-tuple-element.56.mine, f32[1408,256]{1,0:T(8,128)S(1)} %collective-permute-done.7.theirs), custom_call_target="tpu_custom_call" | custom-call | flops 2952790016 | bytes 2883584 | tf_op jit(solution)/shard_map/pallas_call | solution.py:533
  51.6 0.0 collective-permute-done.12.refs_9_
  51.6 0.0 collective-permute-done.11.refs_8_
  51.6 0.0 collective-permute-done.10.refs_7_
  51.6 0.0 collective-permute-done.9.refs_6_
  51.6 0.0 collective-permute-done.8.refs_5_
  51.6 0.0 copy-done.4
  51.7 25.3 %shard_map.102 = (f32[176,352]{1,0:T(8,128)}, f32[352,1024]{1,0:T(8,128)}) custom-call(s32[2]{0:T(128)S(1)} %pad_add_fusion.1.place, f32[1,1408]{1,0:T(1,128)S(1)} %get-tuple-element.37.damping, s32[1,1408]{1,0:T(1,128)S(1)} %get-tuple-element.38.order, bf16[1408,256]{1,0:T(8,128)(2,1)S(1)} %get-tuple-element.57.high, ...), custom_call_target="tpu_custom_call" | custom-call | flops 12180258816 | bytes 9306112 | tf_op jit(solution)/shard_map/pallas_call | solution.py:550
  (1 shorter events, 0.0 us)
Async XLA Ops:
  0.6 1.0 %copy-start = (bf16[128,1024]{1,0:T(8,128)(2,1)S(1)}, bf16[128,1024]{1,0:T(8,128)(2,1)}, u32[]{:S(2)}) copy-start(bf16[128,1024]{1,0:T(8,128)(2,1)} %rx_fields.1) | copy-start | bytes 786436
  1.6 0.9 %copy-start.1 = (bf16[64,1024]{1,0:T(8,128)(2,1)S(1)}, bf16[64,1024]{1,0:T(8,128)(2,1)}, u32[]{:S(2)}) copy-start(bf16[64,1024]{1,0:T(8,128)(2,1)} %tx_fields.1) | copy-start | bytes 393220
  2.5 0.7 copy-start.2
  3.2 10.5 %collective-permute-start.3 = (bf16[208,512]{1,0:T(8,128)(2,1)S(1)}, bf16[208,512]{1,0:T(8,128)(2,1)S(1)}, u32[]{:S(2)}, u32[]{:S(2)}) collective-permute-start(bf16[208,512]{1,0:T(8,128)(2,1)S(1)} %shard_map.95.own), channel_id=1, source_target_pairs={{0,2},{1,3},{2,0},{3,1},{4,6},{5,7},{6,4},{7,5},{8,10},{9,11},{10,... | collective-permute-start | bytes 638984 | tf_op jit(solution)/shard_map/ppermute | solution.py:433
  4.6 9.4 %collective-permute-start.2 = (bf16[208,512]{1,0:T(8,128)(2,1)S(1)}, bf16[208,512]{1,0:T(8,128)(2,1)S(1)}, u32[]{:S(2)}, u32[]{:S(2)}) collective-permute-start(bf16[208,512]{1,0:T(8,128)(2,1)S(1)} %shard_map.95.own), channel_id=1, source_target_pairs={{0,1},{1,0},{2,3},{3,2},{4,5},{5,4},{6,7},{7,6},{8,9},{9,8},{10,11... | collective-permute-start | bytes 638984 | tf_op jit(solution)/shard_map/ppermute | solution.py:433
  5.8 14.3 %collective-permute-start = (bf16[208,512]{1,0:T(8,128)(2,1)S(1)}, bf16[208,512]{1,0:T(8,128)(2,1)S(1)}, u32[]{:S(2)}, u32[]{:S(2)}) collective-permute-start(bf16[208,512]{1,0:T(8,128)(2,1)S(1)} %shard_map.95.own), channel_id=1, source_target_pairs={{0,4},{1,5},{2,6},{3,7},{4,0},{5,1},{6,2},{7,3},{8,12},{9,13},{10,... | collective-permute-start | bytes 638984 | tf_op jit(solution)/shard_map/ppermute | solution.py:433
  5.9 19.4 %collective-permute-start.1 = (bf16[208,512]{1,0:T(8,128)(2,1)S(1)}, bf16[208,512]{1,0:T(8,128)(2,1)S(1)}, u32[]{:S(2)}, u32[]{:S(2)}) collective-permute-start(bf16[208,512]{1,0:T(8,128)(2,1)S(1)} %shard_map.95.own), channel_id=1, source_target_pairs={{0,6},{1,7},{2,4},{3,5},{4,2},{5,3},{6,0},{7,1},{8,14},{9,15},{10,... | collective-permute-start | bytes 638984 | tf_op jit(solution)/shard_map/ppermute | solution.py:433
  10.1 0.7 copy-start.5
  13.8 13.0 %collective-permute-start.6 = (bf16[208,512]{1,0:T(8,128)(2,1)S(1)}, bf16[208,512]{1,0:T(8,128)(2,1)S(1)}, u32[]{:S(2)}, u32[]{:S(2)}) collective-permute-start(bf16[208,512]{1,0:T(8,128)(2,1)S(1)} %collective-permute-done.3.refs_2_), channel_id=1, source_target_pairs={{0,1},{1,0},{2,3},{3,2},{4,5},{5,4},{6,7},{7,6},{8,9},{9,8},{10,11... | collective-permute-start | bytes 638984 | tf_op jit(solution)/shard_map/ppermute | solution.py:433
  25.3 8.4 %collective-permute-start.4 = (bf16[208,512]{1,0:T(8,128)(2,1)S(1)}, bf16[208,512]{1,0:T(8,128)(2,1)S(1)}, u32[]{:S(2)}, u32[]{:S(2)}) collective-permute-start(bf16[208,512]{1,0:T(8,128)(2,1)S(1)} %collective-permute-done.refs_0_), channel_id=1, source_target_pairs={{0,1},{1,0},{2,3},{3,2},{4,5},{5,4},{6,7},{7,6},{8,9},{9,8},{10,11... | collective-permute-start | bytes 638984 | tf_op jit(solution)/shard_map/ppermute | solution.py:433
  25.3 9.5 %collective-permute-start.5 = (bf16[208,512]{1,0:T(8,128)(2,1)S(1)}, bf16[208,512]{1,0:T(8,128)(2,1)S(1)}, u32[]{:S(2)}, u32[]{:S(2)}) collective-permute-start(bf16[208,512]{1,0:T(8,128)(2,1)S(1)} %collective-permute-done.1.refs_1_), channel_id=1, source_target_pairs={{0,1},{1,0},{2,3},{3,2},{4,5},{5,4},{6,7},{7,6},{8,9},{9,8},{10,11... | collective-permute-start | bytes 638984 | tf_op jit(solution)/shard_map/ppermute | solution.py:433
  38.2 7.2 %collective-permute-start.7 = (f32[1408,256]{1,0:T(8,128)S(1)}, f32[1408,256]{1,0:T(8,128)S(1)}, u32[]{:S(2)}, u32[]{:S(2)}) collective-permute-start(f32[1408,256]{1,0:T(8,128)S(1)} %get-tuple-element.56.mine), channel_id=1, source_target_pairs={{0,8},{8,0},{16,24},{24,16},{1,9},{9,1},{17,25},{25,17},{2,10},{10... | collective-permute-start | bytes 4325384 | tf_op jit(solution)/shard_map/ppermute | solution.py:466
  43.6 0.6 copy-start.3
  44.2 7.4 %collective-permute-start.8 = (f32[1152,256]{1,0:T(8,128)}, f32[1152,256]{1,0:T(8,128)}, u32[]{:S(2)}, u32[]{:S(2)}) collective-permute-start(f32[1152,256]{1,0:T(8,128)} %get-tuple-element.65.refs_0_), channel_id=1, source_target_pairs={{0,8},{8,0},{16,24},{24,16},{1,9},{9,1},{17,25},{25,17},{2,10},{10... | collective-permute-start | bytes 3538952 | tf_op jit(solution)/shard_map/ppermute | solution.py:466
  44.2 7.4 %collective-permute-start.9 = (f32[896,256]{1,0:T(8,128)}, f32[896,256]{1,0:T(8,128)}, u32[]{:S(2)}, u32[]{:S(2)}) collective-permute-start(f32[896,256]{1,0:T(8,128)} %get-tuple-element.66.refs_1_), channel_id=1, source_target_pairs={{0,8},{8,0},{16,24},{24,16},{1,9},{9,1},{17,25},{25,17},{2,10},{10... | collective-permute-start | bytes 2752520 | tf_op jit(solution)/shard_map/ppermute | solution.py:466
  44.7 6.9 %collective-permute-start.10 = (f32[640,256]{1,0:T(8,128)S(1)}, f32[640,256]{1,0:T(8,128)}, u32[]{:S(2)}, u32[]{:S(2)}) collective-permute-start(f32[640,256]{1,0:T(8,128)S(1)} %get-tuple-element.67.refs_2_), channel_id=1, source_target_pairs={{0,8},{8,0},{16,24},{24,16},{1,9},{9,1},{17,25},{25,17},{2,10},{10... | collective-permute-start | bytes 1966088 | tf_op jit(solution)/shard_map/ppermute | solution.py:466
  44.8 6.8 %collective-permute-start.11 = (f32[384,256]{1,0:T(8,128)}, f32[384,256]{1,0:T(8,128)}, u32[]{:S(2)}, u32[]{:S(2)}) collective-permute-start(f32[384,256]{1,0:T(8,128)} %get-tuple-element.68.refs_3_), channel_id=1, source_target_pairs={{0,8},{8,0},{16,24},{24,16},{1,9},{9,1},{17,25},{25,17},{2,10},{10... | collective-permute-start | bytes 1179656 | tf_op jit(solution)/shard_map/ppermute | solution.py:466
  45.3 6.3 %collective-permute-start.12 = (f32[128,128]{1,0:T(8,128)}, f32[128,128]{1,0:T(8,128)S(1)}, u32[]{:S(2)}, u32[]{:S(2)}) collective-permute-start(f32[128,128]{1,0:T(8,128)} %copy-done.3), channel_id=1, source_target_pairs={{0,8},{8,0},{16,24},{24,16},{1,9},{9,1},{17,25},{25,17},{2,10},{10... | collective-permute-start | bytes 196616 | tf_op jit(solution)/shard_map/ppermute | solution.py:466
  45.3 6.3 %copy-start.4 = (f32[128,128]{1,0:T(8,128)S(1)}, f32[128,128]{1,0:T(8,128)}, u32[]{:S(2)}) copy-start(f32[128,128]{1,0:T(8,128)} %copy-done.3) | copy-start | bytes 196612

commit v3 on v2

--- a/solution.py
+++ b/solution.py
@@ -182,7 +182,12 @@
         refs[len(strips) + s][...] = refs[s][...] + dot(sens[a:, :], sens[a:b, :], ROWS_ROWS)
 
 
-def gram_body(ntx, nrx, count, stacked, first, some, hot, layer_cond, *refs):
+def sens_body(ntx, nrx, hot, layer_cond, cells, sens, cond):
+    cond[...] = conductivities(ntx, nrx, cells, layer_cond)
+    sensitivities(ntx, nrx, [cells], [cond], hot, sens)
+
+
+def gram_body(ntx, nrx, count, stacked, first, begun, some, hot, layer_cond, *refs):
     held = 1 + first if stacked else count
     blocks, refs = refs[:held], refs[held:]
     rows = hot.shape[0]
@@ -217,9 +222,9 @@
 
         lax.fori_loop(0, count - first, one, 0)
         return
-    if first:
+    if begun:
         sens[:, :size] = blocks[0][...]
-    fill(blocks[first:], size if first else 0)
+    fill(blocks[begun:], size if begun else 0)
     add(None if first else before, count * size)
 
 
@@ -465,11 +470,11 @@
     def swap(value):
         return lax.ppermute(value, "grp", [(i, i ^ 1) for i in range(grp_count)])
 
-    def add(blocks, sums, some=None):
+    def add(blocks, sums, some=None, begun=None):
         count = len(blocks)
         stacked = count > GROUP
         depth = half * (1 if stacked else min(count, GROUP))
-        begun = [] if sums else [own_sens]
+        begun = [] if begun is None else [begun]
         args = [jnp.stack(blocks[len(begun) :])] if stacked else blocks[len(begun) :]
         args = begun + args
         chosen = strips[:some]
@@ -477,7 +482,7 @@
         sens = jax.ShapeDtypeStruct((rows, depth), jnp.bfloat16)
         kept = some is not None
         return pl.pallas_call(
-            functools.partial(gram_body, ntx, nrx, count, stacked, not sums, some),
+            functools.partial(gram_body, ntx, nrx, count, stacked, not sums, len(begun), some),
             in_specs=[VMEM] * (2 + len(args) + len(sums[:some])),
             out_specs=[VMEM] * (len(chosen) + kept),
             out_shape=strip_shapes[:some] + [sens] * kept,
@@ -493,7 +498,7 @@
             ),
         )(hot, conds, *args, *sums[:some])
 
-    sums = list(add([own] + near + far[:1], []))
+    sums = list(add([own] + near + far[:1], [], begun=own_sens))
     held = lax.optimization_barrier((tuple(far[1:]), tuple(sums)))
     far, sums = far[:1] + list(held[0]), list(held[1])
     relayed += [[along(value, (0, k)) for k in range(1, inner)] for value in far[1:]]
@@ -503,7 +508,20 @@
         sums = list(add(blocks, sums))
         theirs = [swap(sums[0])]
     else:
-        one, sens = add(blocks, sums, 1)
+        ready = pl.pallas_call(
+            functools.partial(sens_body, ntx, nrx),
+            in_specs=[VMEM] * 3,
+            out_specs=VMEM,
+            out_shape=jax.ShapeDtypeStruct((rows, half), jnp.bfloat16),
+            scratch_shapes=[pltpu.VMEM((1, half), jnp.float32)],
+            compiler_params=pltpu.CompilerParams(
+                vmem_limit_bytes=grant(((rows, half), 4), ((rows, width), 2))
+            ),
+            cost_estimate=pl.CostEstimate(
+                flops=4 * half * rows * STRIP, bytes_accessed=2 * rows * half, transcendentals=0
+            ),
+        )(hot, conds, blocks[0])
+        one, sens = add(blocks, sums, 1, ready)
         theirs = [swap(one)]
         others = strips[1:]
         sums = [one] + list(

time: 77.3 us -> 76.6 us (level)
  the two profiles are of different devices: /device:TPU:17 before, /device:TPU:0 now
where the time goes in v3:
time: 76.6 us; the launch traced here: 75.6 us
  Pallas kernels  54.1 us (71%)
  starting transfers between devices  11.4 us (15%)
  local copies, waits for them, and re-layouts  6.69 us (9%)
  waiting for transfers between devices  2.48 us (3%)
  between operations  0.79 us (1%)
    pallas_call x1, Pallas kernels, shards(): pl.pallas_call(functools.partial(finish_body, chosen_cols, cell_total, le...  25.3 us
    pallas_call x3, Pallas kernels, add(): pl.pallas_call(functools.partial(gram_body, ntx, nrx, count, stacked, not...  15.5 us
    ppermute x7, starting transfers between devices, along(): return lax.ppermute(value, 'tile', pairs)  9.8 us
    pallas_call x1, Pallas kernels, shards(): pl.pallas_call(functools.partial(start_body, cell_total), in_specs=[VMEM]...  6.23 us
    unnamed x12, local copies, waits for them, and re-layouts  3.86 us
    pallas_call x1, Pallas kernels, shards(): pl.pallas_call(functools.partial(select_body, ntx, nrx), in_specs=[VMEM]...  2.99 us
    pallas_call x1, Pallas kernels, shards(): pl.pallas_call(functools.partial(rest_body, sens.shape[1], others), in_sp...  2.64 us
    ppermute x7, waiting for transfers between devices, along(): return lax.ppermute(value, 'tile', pairs)  2.47 us
  transfers between devices with their start and end apart: 13, of which 1 were waited for; matrix products, arithmetic and copies ran while one was open for 4% of the time, Pallas kernels for 35%

profile of v3, /device:TPU:0, one launch (start us, length us, event | category | flops | bytes accessed | tf_op | source)
XLA Modules:
  0.0 75.6 jit_solution(6108598625263845061)
XLA Ops:
  0.6 0.0 copy-start
  0.6 0.9 %copy-done = bf16[128,1024]{1,0:T(8,128)(2,1)S(1)} copy-done((bf16[128,1024]{1,0:T(8,128)(2,1)S(1)}, bf16[128,1024]{1,0:T(8,128)(2,1)}, u32[]{:S(2)}) %copy-start) | copy-done | bytes 262168
  1.6 0.0 copy-start.1
  1.6 0.9 %copy-done.1 = bf16[64,1024]{1,0:T(8,128)(2,1)S(1)} copy-done((bf16[64,1024]{1,0:T(8,128)(2,1)S(1)}, bf16[64,1024]{1,0:T(8,128)(2,1)}, u32[]{:S(2)}) %copy-start.1) | copy-done | bytes 131096
  2.5 0.0 copy-start.2
  2.5 0.7 copy-done.2
  3.2 0.1 shard_map.95.own
  3.2 3.1 %collective-permute-start.3 = (bf16[208,512]{1,0:T(8,128)(2,1)S(1)}, bf16[208,512]{1,0:T(8,128)(2,1)S(1)}, u32[]{:S(2)}, u32[]{:S(2)}) collective-permute-start(bf16[208,512]{1,0:T(8,128)(2,1)S(1)} %shard_map.95.own), channel_id=1, source_target_pairs={{0,2},{1,3},{2,0},{3,1},{4,6},{5,7},{6,4},{7,5},{8,10},{9,11},{10,... | collective-permute-start | bytes 638984 | tf_op jit(solution)/shard_map/ppermute | solution.py:438
  6.3 1.5 %collective-permute-start.2 = (bf16[208,512]{1,0:T(8,128)(2,1)S(1)}, bf16[208,512]{1,0:T(8,128)(2,1)S(1)}, u32[]{:S(2)}, u32[]{:S(2)}) collective-permute-start(bf16[208,512]{1,0:T(8,128)(2,1)S(1)} %shard_map.95.own), channel_id=1, source_target_pairs={{0,1},{1,0},{2,3},{3,2},{4,5},{5,4},{6,7},{7,6},{8,9},{9,8},{10,11... | collective-permute-start | bytes 638984 | tf_op jit(solution)/shard_map/ppermute | solution.py:438
  7.9 2.6 %collective-permute-start = (bf16[208,512]{1,0:T(8,128)(2,1)S(1)}, bf16[208,512]{1,0:T(8,128)(2,1)S(1)}, u32[]{:S(2)}, u32[]{:S(2)}) collective-permute-start(bf16[208,512]{1,0:T(8,128)(2,1)S(1)} %shard_map.95.own), channel_id=1, source_target_pairs={{0,4},{1,5},{2,6},{3,7},{4,0},{5,1},{6,2},{7,3},{8,12},{9,13},{10,... | collective-permute-start | bytes 638984 | tf_op jit(solution)/shard_map/ppermute | solution.py:438
  10.4 0.2 collective-permute-start.1
  10.7 0.7 stack.24
  11.4 0.7 stack.25
  12.1 0.7 stack.26
  12.8 0.7 broadcast_in_dim.2.layer_cond
  13.5 0.0 copy-start.5
  13.5 0.7 copy-done.5
  14.2 3.0 %shard_map.96 = (bf16[1408,256]{1,0:T(8,128)(2,1)S(1)}, f32[1,1408]{1,0:T(1,128)S(1)}, s32[1,1408]{1,0:T(1,128)S(1)}, bf16[1408,512]{1,0:T(8,128)(2,1)S(1)}) custom-call(s32[3,1408]{1,0:T(4,128)S(1)} %pad_add_fusion.vectors, f32[1408]{0:T(1024)S(1)} %copy-done.5, bf16[208,512]{1,0:T(8,128)(2,1)S(1)} %shard_map.95.own, f32[32,128]{1,0:T(8,128)S(1)} %broadcast_in_dim.2.layer_cond), custom_call_target="tpu_custom_call" | custom-call | flops 1015021568 | bytes 1441792 | tf_op jit(solution)/shard_map/pallas_call | solution.py:447
  17.2 0.0 collective-permute-done.3.refs_2_
  17.2 0.4 collective-permute-start.6
  17.6 0.0 collective-permute-done.2.refs_1_
  17.6 6.0 %shard_map.97 = (f32[1408,256]{1,0:T(8,128)S(1)}, f32[1152,256]{1,0:T(8,128)S(1)}, f32[896,256]{1,0:T(8,128)S(1)}, f32[640,256]{1,0:T(8,128)S(1)}, f32[384,256]{1,0:T(8,128)S(1)}, /*index=5*/f32[128,128]{1,0:T(8,128)S(1)}) custom-call(bf16[1408,256]{1,0:T(8,128)(2,1)S(1)} %get-tuple-element.39.hot, f32[32,128]{1,0:T(8,128)S(1)} %broadcast_in_dim.2.layer_cond, ...), custom_call_target="tpu_custom_call" | custom-call | flops 5788139520 | bytes 9306112 | tf_op jit(solution)/shard_map/pallas_call | solution.py:484
  23.6 2.5 %collective-permute-done.refs_0_ = bf16[208,512]{1,0:T(8,128)(2,1)S(1)} collective-permute-done((bf16[208,512]{1,0:T(8,128)(2,1)S(1)}, bf16[208,512]{1,0:T(8,128)(2,1)S(1)}, u32[]{:S(2)}, u32[]{:S(2)}) %collective-permute-start) | collective-permute-done | bytes 213024 | tf_op jit(solution)/shard_map/ppermute | solution.py:438
  26.1 0.0 collective-permute-done.1.refs_1_
  26.1 0.5 collective-permute-start.4
  26.6 1.5 %collective-permute-start.5 = (bf16[208,512]{1,0:T(8,128)(2,1)S(1)}, bf16[208,512]{1,0:T(8,128)(2,1)S(1)}, u32[]{:S(2)}, u32[]{:S(2)}) collective-permute-start(bf16[208,512]{1,0:T(8,128)(2,1)S(1)} %collective-permute-done.1.refs_1_), channel_id=1, source_target_pairs={{0,1},{1,0},{2,3},{3,2},{4,5},{5,4},{6,7},{7,6},{8,9},{9,8},{10,11... | collective-permute-start | bytes 638984 | tf_op jit(solution)/shard_map/ppermute | solution.py:438
  28.1 0.0 collective-permute-done.6.refs_2_
  28.1 6.9 %shard_map.99 = (f32[1408,256]{1,0:T(8,128)S(1)}, f32[1152,256]{1,0:T(8,128)S(1)}, f32[896,256]{1,0:T(8,128)S(1)}, f32[640,256]{1,0:T(8,128)S(1)}, f32[384,256]{1,0:T(8,128)S(1)}, /*index=5*/f32[128,128]{1,0:T(8,128)S(1)}) custom-call(bf16[1408,256]{1,0:T(8,128)(2,1)S(1)} %get-tuple-element.39.hot, f32[32,128]{1,0:T(8,128)S(1)} %broadcast_in_dim.2.layer_cond, ...), custom_call_target="tpu_custom_call" | custom-call | flops 5788139520 | bytes 9306112 | tf_op jit(solution)/shard_map/pallas_call | solution.py:484
  35.0 0.0 collective-permute-done.4.cells
  35.0 1.4 %shard_map.98.refs_0_ = bf16[1408,512]{1,0:T(8,128)(2,1)S(1)} custom-call(bf16[1408,256]{1,0:T(8,128)(2,1)S(1)} %get-tuple-element.39.hot, f32[32,128]{1,0:T(8,128)S(1)} %broadcast_in_dim.2.layer_cond, bf16[208,512]{1,0:T(8,128)(2,1)S(1)} %collective-permute-done.4.cells), custom_call_target="tpu_custom_call" | custom-call | flops 738197504 | bytes 1441792 | tf_op jit(solution)/shard_map/pallas_call | solution.py:511
  36.5 0.0 collective-permute-done.5.refs_1_
  36.5 2.6 %shard_map.100 = (f32[1408,256]{1,0:T(8,128)S(1)}, bf16[1408,1024]{1,0:T(8,128)(2,1)S(1)}) custom-call(bf16[1408,256]{1,0:T(8,128)(2,1)S(1)} %get-tuple-element.39.hot, f32[32,128]{1,0:T(8,128)S(1)} %broadcast_in_dim.2.layer_cond, bf16[1408,512]{1,0:T(8,128)(2,1)S(1)} %shard_map.98.refs_0_, bf16[208,512]{1,0:T(8,128)(2,1)S(1)} %collective-permute-done.5.refs_1_, ...), custom_call_target="tpu_custom_call" | custom-call | flops 2214592512 | bytes 9306112 | tf_op jit(solution)/shard_map/pallas_call | solution.py:484
  39.1 0.1 collective-permute-start.7
  39.2 2.6 %shard_map.102 = (f32[1152,256]{1,0:T(8,128)}, f32[896,256]{1,0:T(8,128)}, f32[640,256]{1,0:T(8,128)S(1)}, f32[384,256]{1,0:T(8,128)}, f32[128,128]{1,0:T(8,128)S(1)}) custom-call(bf16[1408,1024]{1,0:T(8,128)(2,1)S(1)} %get-tuple-element.59.sens, f32[1152,256]{1,0:T(8,128)S(1)} %get-tuple-element.60.refs_0_, f32[896,256]{1,0:T(8,128)S(1)} %get-tuple-element.61.refs_1_, ...), custom_call_target="tpu_custom_call" | custom-call | flops 2382364672 | bytes 9306112 | tf_op jit(solution)/shard_map/pallas_call | solution.py:528
  41.8 0.0 copy-start.3
  41.8 0.6 copy-done.3
  42.4 0.5 collective-permute-start.8
  42.9 0.0 collective-permute-start.9
  42.9 0.5 collective-permute-start.10
  43.4 0.0 collective-permute-start.11
  43.4 0.1 pad_add_fusion.1.place
  43.5 0.0 collective-permute-done.7.theirs
  43.5 0.5 collective-permute-start.12
  44.0 0.0 copy-start.4
  44.0 6.2 %shard_map.101 = (bf16[1408,256]{1,0:T(8,128)(2,1)S(1)}, bf16[1408,256]{1,0:T(8,128)(2,1)S(1)}) custom-call(f32[1,1408]{1,0:T(1,128)S(1)} %get-tuple-element.37.damping, f32[1408,256]{1,0:T(8,128)S(1)} %get-tuple-element.56.mine, f32[1408,256]{1,0:T(8,128)S(1)} %collective-permute-done.7.theirs), custom_call_target="tpu_custom_call" | custom-call | flops 2952790016 | bytes 2883584 | tf_op jit(solution)/shard_map/pallas_call | solution.py:551
  50.3 0.0 collective-permute-done.12.refs_9_
  50.3 0.0 collective-permute-done.11.refs_8_
  50.3 0.0 collective-permute-done.10.refs_7_
  50.3 0.0 collective-permute-done.9.refs_6_
  50.3 0.0 collective-permute-done.8.refs_5_
  50.3 0.0 copy-done.4
  50.3 25.3 %shard_map.103 = (f32[176,352]{1,0:T(8,128)}, f32[352,1024]{1,0:T(8,128)}) custom-call(s32[2]{0:T(128)S(1)} %pad_add_fusion.1.place, f32[1,1408]{1,0:T(1,128)S(1)} %get-tuple-element.37.damping, s32[1,1408]{1,0:T(1,128)S(1)} %get-tuple-element.38.order, bf16[1408,256]{1,0:T(8,128)(2,1)S(1)} %get-tuple-element.57.high, ...), custom_call_target="tpu_custom_call" | custom-call | flops 12180258816 | bytes 9306112 | tf_op jit(solution)/shard_map/pallas_call | solution.py:568
  (1 shorter events, 0.0 us)
Async XLA Ops:
  0.6 1.0 %copy-start = (bf16[128,1024]{1,0:T(8,128)(2,1)S(1)}, bf16[128,1024]{1,0:T(8,128)(2,1)}, u32[]{:S(2)}) copy-start(bf16[128,1024]{1,0:T(8,128)(2,1)} %rx_fields.1) | copy-start | bytes 786436
  1.6 0.9 %copy-start.1 = (bf16[64,1024]{1,0:T(8,128)(2,1)S(1)}, bf16[64,1024]{1,0:T(8,128)(2,1)}, u32[]{:S(2)}) copy-start(bf16[64,1024]{1,0:T(8,128)(2,1)} %tx_fields.1) | copy-start | bytes 393220
  2.5 0.7 copy-start.2
  3.2 14.0 %collective-permute-start.3 = (bf16[208,512]{1,0:T(8,128)(2,1)S(1)}, bf16[208,512]{1,0:T(8,128)(2,1)S(1)}, u32[]{:S(2)}, u32[]{:S(2)}) collective-permute-start(bf16[208,512]{1,0:T(8,128)(2,1)S(1)} %shard_map.95.own), channel_id=1, source_target_pairs={{0,2},{1,3},{2,0},{3,1},{4,6},{5,7},{6,4},{7,5},{8,10},{9,11},{10,... | collective-permute-start | bytes 638984 | tf_op jit(solution)/shard_map/ppermute | solution.py:438
  6.3 11.2 %collective-permute-start.2 = (bf16[208,512]{1,0:T(8,128)(2,1)S(1)}, bf16[208,512]{1,0:T(8,128)(2,1)S(1)}, u32[]{:S(2)}, u32[]{:S(2)}) collective-permute-start(bf16[208,512]{1,0:T(8,128)(2,1)S(1)} %shard_map.95.own), channel_id=1, source_target_pairs={{0,1},{1,0},{2,3},{3,2},{4,5},{5,4},{6,7},{7,6},{8,9},{9,8},{10,11... | collective-permute-start | bytes 638984 | tf_op jit(solution)/shard_map/ppermute | solution.py:438
  7.9 18.2 %collective-permute-start = (bf16[208,512]{1,0:T(8,128)(2,1)S(1)}, bf16[208,512]{1,0:T(8,128)(2,1)S(1)}, u32[]{:S(2)}, u32[]{:S(2)}) collective-permute-start(bf16[208,512]{1,0:T(8,128)(2,1)S(1)} %shard_map.95.own), channel_id=1, source_target_pairs={{0,4},{1,5},{2,6},{3,7},{4,0},{5,1},{6,2},{7,3},{8,12},{9,13},{10,... | collective-permute-start | bytes 638984 | tf_op jit(solution)/shard_map/ppermute | solution.py:438
  10.4 15.6 %collective-permute-start.1 = (bf16[208,512]{1,0:T(8,128)(2,1)S(1)}, bf16[208,512]{1,0:T(8,128)(2,1)S(1)}, u32[]{:S(2)}, u32[]{:S(2)}) collective-permute-start(bf16[208,512]{1,0:T(8,128)(2,1)S(1)} %shard_map.95.own), channel_id=1, source_target_pairs={{0,6},{1,7},{2,4},{3,5},{4,2},{5,3},{6,0},{7,1},{8,14},{9,15},{10,... | collective-permute-start | bytes 638984 | tf_op jit(solution)/shard_map/ppermute | solution.py:438
  13.5 0.7 copy-start.5
  17.2 10.9 %collective-permute-start.6 = (bf16[208,512]{1,0:T(8,128)(2,1)S(1)}, bf16[208,512]{1,0:T(8,128)(2,1)S(1)}, u32[]{:S(2)}, u32[]{:S(2)}) collective-permute-start(bf16[208,512]{1,0:T(8,128)(2,1)S(1)} %collective-permute-done.3.refs_2_), channel_id=1, source_target_pairs={{0,1},{1,0},{2,3},{3,2},{4,5},{5,4},{6,7},{7,6},{8,9},{9,8},{10,11... | collective-permute-start | bytes 638984 | tf_op jit(solution)/shard_map/ppermute | solution.py:438
  26.1 9.0 %collective-permute-start.4 = (bf16[208,512]{1,0:T(8,128)(2,1)S(1)}, bf16[208,512]{1,0:T(8,128)(2,1)S(1)}, u32[]{:S(2)}, u32[]{:S(2)}) collective-permute-start(bf16[208,512]{1,0:T(8,128)(2,1)S(1)} %collective-permute-done.refs_0_), channel_id=1, source_target_pairs={{0,1},{1,0},{2,3},{3,2},{4,5},{5,4},{6,7},{7,6},{8,9},{9,8},{10,11... | collective-permute-start | bytes 638984 | tf_op jit(solution)/shard_map/ppermute | solution.py:438
  26.6 9.9 %collective-permute-start.5 = (bf16[208,512]{1,0:T(8,128)(2,1)S(1)}, bf16[208,512]{1,0:T(8,128)(2,1)S(1)}, u32[]{:S(2)}, u32[]{:S(2)}) collective-permute-start(bf16[208,512]{1,0:T(8,128)(2,1)S(1)} %collective-permute-done.1.refs_1_), channel_id=1, source_target_pairs={{0,1},{1,0},{2,3},{3,2},{4,5},{5,4},{6,7},{7,6},{8,9},{9,8},{10,11... | collective-permute-start | bytes 638984 | tf_op jit(solution)/shard_map/ppermute | solution.py:438
  39.1 4.4 %collective-permute-start.7 = (f32[1408,256]{1,0:T(8,128)S(1)}, f32[1408,256]{1,0:T(8,128)S(1)}, u32[]{:S(2)}, u32[]{:S(2)}) collective-permute-start(f32[1408,256]{1,0:T(8,128)S(1)} %get-tuple-element.56.mine), channel_id=1, source_target_pairs={{0,8},{8,0},{16,24},{24,16},{1,9},{9,1},{17,25},{25,17},{2,10},{10... | collective-permute-start | bytes 4325384 | tf_op jit(solution)/shard_map/ppermute | solution.py:471
  41.8 0.6 copy-start.3
  42.4 7.9 %collective-permute-start.8 = (f32[1152,256]{1,0:T(8,128)}, f32[1152,256]{1,0:T(8,128)}, u32[]{:S(2)}, u32[]{:S(2)}) collective-permute-start(f32[1152,256]{1,0:T(8,128)} %get-tuple-element.65.refs_0_), channel_id=1, source_target_pairs={{0,8},{8,0},{16,24},{24,16},{1,9},{9,1},{17,25},{25,17},{2,10},{10... | collective-permute-start | bytes 3538952 | tf_op jit(solution)/shard_map/ppermute | solution.py:471
  42.9 7.4 %collective-permute-start.9 = (f32[896,256]{1,0:T(8,128)}, f32[896,256]{1,0:T(8,128)}, u32[]{:S(2)}, u32[]{:S(2)}) collective-permute-start(f32[896,256]{1,0:T(8,128)} %get-tuple-element.66.refs_1_), channel_id=1, source_target_pairs={{0,8},{8,0},{16,24},{24,16},{1,9},{9,1},{17,25},{25,17},{2,10},{10... | collective-permute-start | bytes 2752520 | tf_op jit(solution)/shard_map/ppermute | solution.py:471
  42.9 7.3 %collective-permute-start.10 = (f32[640,256]{1,0:T(8,128)S(1)}, f32[640,256]{1,0:T(8,128)}, u32[]{:S(2)}, u32[]{:S(2)}) collective-permute-start(f32[640,256]{1,0:T(8,128)S(1)} %get-tuple-element.67.refs_2_), channel_id=1, source_target_pairs={{0,8},{8,0},{16,24},{24,16},{1,9},{9,1},{17,25},{25,17},{2,10},{10... | collective-permute-start | bytes 1966088 | tf_op jit(solution)/shard_map/ppermute | solution.py:471
  43.4 6.8 %collective-permute-start.11 = (f32[384,256]{1,0:T(8,128)}, f32[384,256]{1,0:T(8,128)}, u32[]{:S(2)}, u32[]{:S(2)}) collective-permute-start(f32[384,256]{1,0:T(8,128)} %get-tuple-element.68.refs_3_), channel_id=1, source_target_pairs={{0,8},{8,0},{16,24},{24,16},{1,9},{9,1},{17,25},{25,17},{2,10},{10... | collective-permute-start | bytes 1179656 | tf_op jit(solution)/shard_map/ppermute | solution.py:471
  43.5 6.7 %collective-permute-start.12 = (f32[128,128]{1,0:T(8,128)}, f32[128,128]{1,0:T(8,128)S(1)}, u32[]{:S(2)}, u32[]{:S(2)}) collective-permute-start(f32[128,128]{1,0:T(8,128)} %copy-done.3), channel_id=1, source_target_pairs={{0,8},{8,0},{16,24},{24,16},{1,9},{9,1},{17,25},{25,17},{2,10},{10... | collective-permute-start | bytes 196616 | tf_op jit(solution)/shard_map/ppermute | solution.py:471
  44.0 6.3 %copy-start.4 = (f32[128,128]{1,0:T(8,128)S(1)}, f32[128,128]{1,0:T(8,128)}, u32[]{:S(2)}) copy-start(f32[128,128]{1,0:T(8,128)} %copy-done.3) | copy-start | bytes 196612
